TPU v7x, 32 devices: a whole 2x2x4 slice. The times are simulated.
32 devices in a mesh: lon: 16 (over z, y, x), lat: 2 (over core).
Axes of the slice: x: 2, y: 2, z: 4, core: 2. Of those that a mesh axis runs over, the one named last changes fastest.
Arguments:
- potential_heat: float32 [4, 192, 2048], P(None, 'lat', 'lon'), may hold values from -6 to 6
- salt_anomaly_field: float32 [4, 192, 2048], P(None, 'lat', 'lon'), may hold values from -6 to 6
- zonal_current: float32 [4, 192, 2048], P(None, 'lat', 'lon'), may hold values from -6 to 6
- meridional_current: float32 [4, 192, 2048], P(None, 'lat', 'lon'), may hold values from -6 to 6
- water_indicator: int32 [4, 192, 2048], P(None, 'lat', 'lon'), may hold values 0 or 1
- floor_layer_index: int32 [192, 2048], P('lat', 'lon'), may hold values from 0 to 3
- zonal_spacing: float32 [192, 2048], P('lat', 'lon'), may hold values from 0.7 to 1.4
- meridional_spacing: float32 [192, 2048], P('lat', 'lon'), may hold values from 0.7 to 1.4
- planetary_rotation_factor: float32 [192, 2048], P('lat', 'lon'), may hold values from 0.3 to 1.5
- horizontal_eddy_coefficient: float32 [192, 2048], P('lat', 'lon'), may hold values from 0.05 to 0.25
- diapycnal_diffusivity: float32 [3, 192, 2048], P(None, 'lat', 'lon'), may hold values from 0.02 to 0.5
- layer_height: float32 [4], replicated, may hold values from 0.7 to 1.4
Outputs:
- new_temperature: float32 [4, 192, 2048], P(None, 'lat', 'lon')
- new_salinity: float32 [4, 192, 2048], P(None, 'lat', 'lon')
- new_zonal: float32 [4, 192, 2048], P(None, 'lat', 'lon')
- new_meridional: float32 [4, 192, 2048], P(None, 'lat', 'lon')
All inputs are finite; a program needn't handle non-finite values. No bound on the sum of `water_indicator` on one device may be relied on, other than what follows from the above.
Results may differ from a plain program's by a relative error of at most 0.0003.
Values sent between devices are 32-bit elements; how exact they have to be, the bound alone decides.
A program may use at most 64 MiB of HBM per device.

v0:
```python
import jax
import jax.numpy as jnp
from jax import lax
from jax.sharding import PartitionSpec as P

TIME_STEP = 0.25
EXPANSION = 0.2
CONTRACTION = 0.8
BOTTOM_DRAG = 1.0


def with_halo(value, sides, width, wrap):
    for axis, dim in sides:
        size, length = (lax.axis_size(axis), value.shape[dim])
        up = [(i, (i + 1) % size) for i in range(size if wrap else size - 1)]
        down = [(j, i) for i, j in up]
        last = lax.slice_in_dim(value, length - width, length, axis=dim)
        leading = lax.slice_in_dim(value, 0, width, axis=dim)
        before = lax.ppermute(last, axis, up)
        after = lax.ppermute(leading, axis, down)
        value = jnp.concatenate([before, value, after], axis=dim)
    return value


def pressure(temp_part, salt_part, layer_height):
    layer_mass = (CONTRACTION * salt_part - EXPANSION * temp_part) * layer_height[:, None, None]
    return jnp.cumsum(layer_mass, axis=0) - 0.5 * layer_mass


def mix_vertically(fields, water_share, diapycnal_diffusivity, layer_height):
    contrast = fields[:, 1:] - fields[:, :-1]
    fluxes = diapycnal_diffusivity * (water_share[1:] * water_share[:-1]) * contrast
    boundary = jnp.zeros_like(fluxes[:, :1])
    flux_below = jnp.concatenate([fluxes, boundary], axis=1)
    flux_above = jnp.concatenate([boundary, fluxes], axis=1)
    return (flux_below - flux_above) / (layer_height * layer_height)[None, :, None, None]


def advance(
    central,
    eastern,
    western,
    northern,
    southern,
    at_bottom,
    zonal_spacing,
    meridional_spacing,
    planetary_rotation_factor,
    horizontal_eddy_coefficient,
    diapycnal_diffusivity,
    layer_height,
):
    water_share = central[4]
    fields = central[:4]
    weight_east = water_share * eastern[4]
    weight_west = water_share * western[4]
    weight_north = water_share * northern[4]
    weight_south = water_share * southern[4]
    diffusion = horizontal_eddy_coefficient * (
        (weight_east * (eastern[:4] - fields) + weight_west * (western[:4] - fields))
        / (zonal_spacing * zonal_spacing)
        + (weight_north * (northern[:4] - fields) + weight_south * (southern[:4] - fields))
        / (meridional_spacing * meridional_spacing)
    )
    zonal = fields[2]
    merid = fields[3]
    advection = -(
        zonal * (eastern[:4] - western[:4]) * (0.5 / zonal_spacing)
        + merid * (northern[:4] - southern[:4]) * (0.5 / meridional_spacing)
    )
    pressure_east = pressure(eastern[0], eastern[1], layer_height)
    pressure_west = pressure(western[0], western[1], layer_height)
    pressure_north = pressure(northern[0], northern[1], layer_height)
    pressure_south = pressure(southern[0], southern[1], layer_height)
    gradient_x = -(pressure_east - pressure_west) * (0.5 / zonal_spacing)
    gradient_y = -(pressure_north - pressure_south) * (0.5 / meridional_spacing)
    mixing = mix_vertically(fields, water_share, diapycnal_diffusivity, layer_height)
    tendency = advection + diffusion + mixing
    tend_zonal = (
        tendency[2]
        + planetary_rotation_factor * merid
        + gradient_x
        - BOTTOM_DRAG * at_bottom * zonal
    )
    tend_merid = (
        tendency[3]
        - planetary_rotation_factor * zonal
        + gradient_y
        - BOTTOM_DRAG * at_bottom * merid
    )
    tendency = jnp.stack([tendency[0], tendency[1], tend_zonal, tend_merid])
    updated = water_share * (fields + TIME_STEP * tendency)
    return jnp.concatenate([updated, water_share[None]], axis=0)


def fold_ghost(top_row):
    fold_sign = jnp.array([1.0, 1.0, -1.0, -1.0, 1.0], jnp.float32).reshape(5, 1, 1)
    row_width = top_row.shape[2]
    gathered = lax.all_gather(top_row, "lon", axis=2, tiled=True)
    partner = lax.axis_size("lon") - 1 - lax.axis_index("lon")
    mirrored = lax.dynamic_slice_in_dim(gathered, partner * row_width, row_width, 2)
    return mirrored[:, :, ::-1] * fold_sign


def shards(
    potential_heat,
    salt_anomaly_field,
    zonal_current,
    meridional_current,
    water_indicator,
    floor_layer_index,
    zonal_spacing,
    meridional_spacing,
    planetary_rotation_factor,
    horizontal_eddy_coefficient,
    diapycnal_diffusivity,
    layer_height,
):
    water_share = water_indicator.astype(jnp.float32)
    combined_tracers = jnp.stack(
        [
            potential_heat * water_share,
            salt_anomaly_field * water_share,
            zonal_current * water_share,
            meridional_current * water_share,
            water_share,
        ]
    )
    levels = combined_tracers.shape[1]
    is_top = lax.axis_index("lat") == lax.axis_size("lat") - 1
    at_bottom = (
        lax.broadcasted_iota(jnp.int32, (levels, 1, 1), 0) == floor_layer_index[None]
    ).astype(jnp.float32)
    for step_index in range(2):
        lon_padded = with_halo(combined_tracers, (("lon", 3),), 1, True)
        lat_padded = with_halo(combined_tracers, (("lat", 2),), 1, False)
        ghost_row = fold_ghost(combined_tracers[:, :, -1, :])
        north_rim = jnp.where(is_top, ghost_row, lat_padded[:, :, -1, :])
        northern = jnp.concatenate([lat_padded[:, :, 2:-1, :], north_rim[:, :, None, :]], axis=2)
        southern = lat_padded[:, :, :-2, :]
        eastern = lon_padded[..., 2:]
        western = lon_padded[..., :-2]
        combined_tracers = advance(
            combined_tracers,
            eastern,
            western,
            northern,
            southern,
            at_bottom,
            zonal_spacing,
            meridional_spacing,
            planetary_rotation_factor,
            horizontal_eddy_coefficient,
            diapycnal_diffusivity,
            layer_height,
        )
    return (combined_tracers[0], combined_tracers[1], combined_tracers[2], combined_tracers[3])


def solution(mesh):
    return jax.shard_map(
        shards,
        mesh=mesh,
        in_specs=(
            P(None, "lat", "lon"),
            P(None, "lat", "lon"),
            P(None, "lat", "lon"),
            P(None, "lat", "lon"),
            P(None, "lat", "lon"),
            P("lat", "lon"),
            P("lat", "lon"),
            P("lat", "lon"),
            P("lat", "lon"),
            P("lat", "lon"),
            P(None, "lat", "lon"),
            P(),
        ),
        out_specs=(
            P(None, "lat", "lon"),
            P(None, "lat", "lon"),
            P(None, "lat", "lon"),
            P(None, "lat", "lon"),
        ),
        check_vma=False,
    )
```

profile of v0, /device:TPU:0, one launch (start us, length us, event | category | flops | bytes accessed | tf_op | source)
XLA Modules:
  0.0 138.6 jit_solution(707916303006285761)
XLA Ops:
  0.7 1.1 constant_dynamic-update-slice_fusion.4
  1.8 1.1 constant_dynamic-update-slice_fusion.3
  2.9 1.1 constant_dynamic-update-slice_fusion.2
  4.7 1.3 collective-permute-start.2
  6.0 3.6 %collective-permute-start.3 = (f32[5,4,1,128]{3,2,1,0:T(1,128)}, f32[5,4,1,128]{3,2,1,0:T(1,128)S(1)}, u32[]{:S(2)}, u32[]{:S(2)}) collective-permute-start(f32[5,4,1,128]{3,2,1,0:T(1,128)} %get-tuple-element.27), channel_id=1, source_target_pairs={{0,1},{2,3},{4,5},{6,7},{8,9},{10,11},{12,13},{14,15},{16,17},{18,... | collective-permute-start | bytes 30728 | tf_op jit(solution)/shard_map/ppermute | solution.py:19
  9.6 1.3 fusion.149
  10.9 2.2 %copy.83 = f32[5,4,96,1]{2,1,3,0:T(4,128)} copy(f32[5,4,96,1]{3,2,1,0:T(8,128)} %get-tuple-element.25) | data formatting | bytes 15360 | tf_op jit(solution)/shard_map/slice | solution.py:18
  13.1 6.9 %collective-permute-start = (f32[5,4,96,1]{2,1,3,0:T(4,128)}, f32[5,4,96,1]{2,1,3,0:T(4,128)}, u32[]{:S(2)}, u32[]{:S(2)}) collective-permute-start(f32[5,4,96,1]{2,1,3,0:T(4,128)} %copy.83), channel_id=1, source_target_pairs={{2,0},{4,2},{6,4},{8,6},{10,8},{12,10},{14,12},{16,14},{18,16},{20... | collective-permute-start | bytes 23048 | tf_op jit(solution)/shard_map/ppermute | solution.py:20
  20.4 42.2 %all-gather = f32[5,4,1,2048]{3,2,1,0:T(1,128)S(1)} all-gather(f32[5,4,1,128]{3,2,1,0:T(1,128)} %get-tuple-element.27), channel_id=2, replica_groups=mesh['lon'=16,'lat'=2] {'lon'}, dimensions={3}, use_global_device_ids=true | all-gather | bytes 174080 | tf_op jit(solution)/shard_map/all_gather | solution.py:99
  65.8 1.1 copy.86
  67.8 2.0 %copy.84 = f32[5,4,96,1]{3,2,1,0:T(8,128)} copy(f32[5,4,96,1]{2,1,3,0:T(4,128)} %collective-permute-done) | data formatting | bytes 15360 | tf_op jit(solution)/shard_map/ppermute | solution.py:20
  70.7 1.4 fusion.74
  72.4 1.3 divide_add_fusion.1
  75.5 1.3 fusion.22
  76.9 38.6 %all-gather.1 = f32[5,4,1,2048]{3,2,1,0:T(1,128)} all-gather(f32[5,4,1,128]{3,2,1,0:T(1,128)S(1)} %get-tuple-element.23), channel_id=3, replica_groups=mesh['lon'=16,'lat'=2] {'lon'}, dimensions={3}, use_global_device_ids=true | all-gather | bytes 174080 | tf_op jit(solution)/shard_map/all_gather | solution.py:99
  115.5 1.3 collective-permute-start.7
  118.5 1.5 %copy.91 = f32[5,4,96,1]{2,1,3,0:T(4,128)S(1)} copy(f32[5,4,96,1]{3,2,1,0:T(8,128)} %get-tuple-element.21) | data formatting | bytes 15360 | tf_op jit(solution)/shard_map/slice | solution.py:17
  120.1 2.0 %collective-permute-start.5 = (f32[5,4,96,1]{2,1,3,0:T(4,128)S(1)}, f32[5,4,96,1]{2,1,3,0:T(4,128)S(1)}, u32[]{:S(2)}, u32[]{:S(2)}) collective-permute-start(f32[5,4,96,1]{2,1,3,0:T(4,128)S(1)} %copy.91), channel_id=1, source_target_pairs={{0,2},{2,4},{4,6},{6,8},{8,10},{10,12},{12,14},{14,16},{16,18},{18... | collective-permute-start | bytes 23048 | tf_op jit(solution)/shard_map/ppermute | solution.py:19
  122.4 3.6 %collective-permute-start.4 = (f32[5,4,96,1]{2,1,3,0:T(4,128)S(1)}, f32[5,4,96,1]{2,1,3,0:T(4,128)S(1)}, u32[]{:S(2)}, u32[]{:S(2)}) collective-permute-start(f32[5,4,96,1]{2,1,3,0:T(4,128)S(1)} %copy.89), channel_id=1, source_target_pairs={{2,0},{4,2},{6,4},{8,6},{10,8},{12,10},{14,12},{16,14},{18,16},{20... | collective-permute-start | bytes 23048 | tf_op jit(solution)/shard_map/ppermute | solution.py:20
  126.9 1.3 collective-permute-start.6
  128.5 1.0 reduce-window_subtract_fusion.2
  129.5 1.3 copy.90
  130.9 1.9 %pad_maximum_fusion = (f32[5,4,96,129]{3,2,1,0:T(8,128)S(1)}, f32[5,4,96,129]{3,2,1,0:T(8,128)S(1)}) fusion(f32[5,4,96,1]{3,2,1,0:T(8,128)} %copy.90, f32[1,4,96,128]{3,2,1,0:T(8,128)S(1)} %get-tuple-element.35, f32[4,4,96,128]{3,2,1,0:T(8,128)S(1)} %fusion.31, f32[5,4,96,1]{3,2,1,0:T(8,128)S(1)} %copy.92), kind=kLoop, calls=%fused_computation.19 | loop fusion | flops 990720 | bytes 2979840 | tf_op jit(solution)/shard_map/concatenate | solution.py:21
  133.0 1.0 copy-done.1
  (144 shorter events, 15.8 us)
Async XLA Ops:
  0.6 3.4 %copy-start.2 = (s32[4,96,128]{2,1,0:T(8,128)S(1)}, s32[4,96,128]{2,1,0:T(8,128)}, u32[]{:S(2)}) copy-start(s32[4,96,128]{2,1,0:T(8,128)} %param.18) | copy-start | bytes 589828
  0.6 3.4 %copy-start.41 = (f32[4,96,128]{2,1,0:T(8,128)S(1)}, f32[4,96,128]{2,1,0:T(8,128)}, u32[]{:S(2)}) copy-start(f32[4,96,128]{2,1,0:T(8,128)} %param.17) | copy-start | bytes 589828
  1.8 60.9 %copy-start.4 = (f32[1,4,96,128]{3,2,1,0:T(8,128)}, f32[1,4,96,128]{3,2,1,0:T(8,128)S(1)}, u32[]{:S(2)}) copy-start(f32[1,4,96,128]{3,2,1,0:T(8,128)S(1)} %get-tuple-element.11) | copy-start | bytes 589828
  2.9 59.8 %copy-start.7 = (f32[1,4,96,128]{3,2,1,0:T(8,128)}, f32[1,4,96,128]{3,2,1,0:T(8,128)S(1)}, u32[]{:S(2)}) copy-start(f32[1,4,96,128]{3,2,1,0:T(8,128)S(1)} %get-tuple-element.9) | copy-start | bytes 589828
  4.7 65.1 %collective-permute-start.2 = (f32[5,4,1,128]{3,1,0,2:T(4,128)}, f32[5,4,1,128]{3,1,0,2:T(4,128)}, u32[]{:S(2)}, u32[]{:S(2)}) collective-permute-start(f32[5,4,1,128]{3,1,0,2:T(4,128)} %bitcast.37), channel_id=1, source_target_pairs={{1,0},{3,2},{5,4},{7,6},{9,8},{11,10},{13,12},{15,14},{17,16},{19,... | collective-permute-start | bytes 30728 | tf_op jit(solution)/shard_map/ppermute | solution.py:20
  6.0 64.6 %collective-permute-start.3 = (f32[5,4,1,128]{3,2,1,0:T(1,128)}, f32[5,4,1,128]{3,2,1,0:T(1,128)S(1)}, u32[]{:S(2)}, u32[]{:S(2)}) collective-permute-start(f32[5,4,1,128]{3,2,1,0:T(1,128)} %get-tuple-element.27), channel_id=1, source_target_pairs={{0,1},{2,3},{4,5},{6,7},{8,9},{10,11},{12,13},{14,15},{16,17},{18,... | collective-permute-start | bytes 30728 | tf_op jit(solution)/shard_map/ppermute | solution.py:19
  10.9 51.7 %copy-start.42 = (f32[3,96,128]{2,1,0:T(8,128)S(1)}, f32[3,96,128]{2,1,0:T(8,128)}, u32[]{:S(2)}) copy-start(f32[3,96,128]{2,1,0:T(8,128)} %param.24) | copy-start | bytes 442372
  13.1 54.7 %collective-permute-start = (f32[5,4,96,1]{2,1,3,0:T(4,128)}, f32[5,4,96,1]{2,1,3,0:T(4,128)}, u32[]{:S(2)}, u32[]{:S(2)}) collective-permute-start(f32[5,4,96,1]{2,1,3,0:T(4,128)} %copy.83), channel_id=1, source_target_pairs={{2,0},{4,2},{6,4},{8,6},{10,8},{12,10},{14,12},{16,14},{18,16},{20... | collective-permute-start | bytes 23048 | tf_op jit(solution)/shard_map/ppermute | solution.py:20
  20.4 45.4 %collective-permute-start.1 = (f32[5,4,96,1]{2,1,3,0:T(4,128)S(1)}, f32[5,4,96,1]{2,1,3,0:T(4,128)}, u32[]{:S(2)}, u32[]{:S(2)}) collective-permute-start(f32[5,4,96,1]{2,1,3,0:T(4,128)S(1)} %copy.85), channel_id=1, source_target_pairs={{0,2},{2,4},{4,6},{6,8},{8,10},{10,12},{12,14},{14,16},{16,18},{18... | collective-permute-start | bytes 23048 | tf_op jit(solution)/shard_map/ppermute | solution.py:19
  62.7 1.7 %copy-start.21 = (f32[3,96,128]{2,1,0:T(8,128)}, f32[3,96,128]{2,1,0:T(8,128)S(1)}, u32[]{:S(2)}) copy-start(f32[3,96,128]{2,1,0:T(8,128)S(1)} %fusion.99) | copy-start | bytes 442372
  62.8 2.4 %copy-start.43 = (f32[4]{0:T(128)S(1)}, f32[4]{0:T(128)}, u32[]{:S(2)}) copy-start(f32[4]{0:T(128)} %param.25) | copy-start | bytes 52
  70.7 1.6 %copy-start.19 = (f32[4,3,96,128]{3,2,1,0:T(8,128)S(1)}, f32[4,3,96,128]{3,2,1,0:T(8,128)}, u32[]{:S(2)}) copy-start(f32[4,3,96,128]{3,2,1,0:T(8,128)} %fusion.35) | copy-start | bytes 1769476
  70.7 1.6 %copy-start.23 = (f32[96,128]{1,0:T(8,128)S(1)}, f32[96,128]{1,0:T(8,128)}, u32[]{:S(2)}) copy-start(f32[96,128]{1,0:T(8,128)} %get-tuple-element.43) | copy-start | bytes 147460
  70.7 1.6 %copy-start.25 = (f32[96,128]{1,0:T(8,128)S(1)}, f32[96,128]{1,0:T(8,128)}, u32[]{:S(2)}) copy-start(f32[96,128]{1,0:T(8,128)} %get-tuple-element.40) | copy-start | bytes 147460
  70.7 1.6 %copy-start.35 = (f32[96,128]{1,0:T(8,128)S(1)}, f32[96,128]{1,0:T(8,128)}, u32[]{:S(2)}) copy-start(f32[96,128]{1,0:T(8,128)} %get-tuple-element.41) | copy-start | bytes 147460
  76.8 40.1 %copy-start.22 = (f32[3,96,128]{2,1,0:T(8,128)S(1)}, f32[3,96,128]{2,1,0:T(8,128)}, u32[]{:S(2)}) copy-start(f32[3,96,128]{2,1,0:T(8,128)} %copy-done.21) | copy-start | bytes 442372
  115.5 17.3 %collective-permute-start.7 = (f32[5,4,1,128]{3,2,1,0:T(1,128)S(1)}, f32[5,4,1,128]{3,2,1,0:T(1,128)S(1)}, u32[]{:S(2)}, u32[]{:S(2)}) collective-permute-start(f32[5,4,1,128]{3,2,1,0:T(1,128)S(1)} %get-tuple-element.23), channel_id=1, source_target_pairs={{0,1},{2,3},{4,5},{6,7},{8,9},{10,11},{12,13},{14,15},{16,17},{18,... | collective-permute-start | bytes 30728 | tf_op jit(solution)/shard_map/ppermute | solution.py:19
  120.1 8.1 %collective-permute-start.5 = (f32[5,4,96,1]{2,1,3,0:T(4,128)S(1)}, f32[5,4,96,1]{2,1,3,0:T(4,128)S(1)}, u32[]{:S(2)}, u32[]{:S(2)}) collective-permute-start(f32[5,4,96,1]{2,1,3,0:T(4,128)S(1)} %copy.91), channel_id=1, source_target_pairs={{0,2},{2,4},{4,6},{6,8},{8,10},{10,12},{12,14},{14,16},{16,18},{18... | collective-permute-start | bytes 23048 | tf_op jit(solution)/shard_map/ppermute | solution.py:19
  122.4 7.1 %collective-permute-start.4 = (f32[5,4,96,1]{2,1,3,0:T(4,128)S(1)}, f32[5,4,96,1]{2,1,3,0:T(4,128)S(1)}, u32[]{:S(2)}, u32[]{:S(2)}) collective-permute-start(f32[5,4,96,1]{2,1,3,0:T(4,128)S(1)} %copy.89), channel_id=1, source_target_pairs={{2,0},{4,2},{6,4},{8,6},{10,8},{12,10},{14,12},{16,14},{18,16},{20... | collective-permute-start | bytes 23048 | tf_op jit(solution)/shard_map/ppermute | solution.py:20
  126.9 5.9 %collective-permute-start.6 = (f32[5,4,1,128]{3,2,1,0:T(1,128)S(1)}, f32[5,4,1,128]{3,2,1,0:T(1,128)S(1)}, u32[]{:S(2)}, u32[]{:S(2)}) collective-permute-start(f32[5,4,1,128]{3,2,1,0:T(1,128)S(1)} %get-tuple-element.22), channel_id=1, source_target_pairs={{1,0},{3,2},{5,4},{7,6},{9,8},{11,10},{13,12},{15,14},{17,16},{19,... | collective-permute-start | bytes 30728 | tf_op jit(solution)/shard_map/ppermute | solution.py:20
  130.9 1.9 %copy-start.46 = (f32[5]{0:T(128)S(1)}, f32[5]{0:T(128)}, u32[]{:S(2)}) copy-start(f32[5]{0:T(128)} %constant.45.clone) | copy-start | bytes 64
  134.1 1.6 %copy-start.34 = (f32[4,96,128]{2,1,0:T(8,128)S(1)}, f32[4,96,128]{2,1,0:T(8,128)}, u32[]{:S(2)}) copy-start(f32[4,96,128]{2,1,0:T(8,128)} %get-tuple-element.33) | copy-start | bytes 589828
  134.1 1.6 %copy-start.36 = (f32[96,128]{1,0:T(8,128)S(1)}, f32[96,128]{1,0:T(8,128)}, u32[]{:S(2)}) copy-start(f32[96,128]{1,0:T(8,128)} %get-tuple-element.41) | copy-start | bytes 147460
  134.1 1.6 %copy-start.38 = (f32[96,128]{1,0:T(8,128)S(1)}, f32[96,128]{1,0:T(8,128)}, u32[]{:S(2)}) copy-start(f32[96,128]{1,0:T(8,128)} %get-tuple-element.42) | copy-start | bytes 147460
  (33 other events, 42.2 us)
where the time goes:
time: 140 us; the launch traced here: 139 us
  blocking collectives  80.8 us (58%)
  starting transfers between devices  20.1 us (14%)
  other arithmetic  18.5 us (13%)
  local copies, waits for them, and re-layouts  17.8 us (13%)
    all_gather x2, blocking collectives, fold_ghost(): gathered = lax.all_gather(top_row, 'lon', axis=2, tiled=True)  80.8 us
    ppermute x4, starting transfers between devices, with_halo(): after = lax.ppermute(leading, axis, down)  13.1 us
    ppermute x4, starting transfers between devices, with_halo(): before = lax.ppermute(last, axis, up)  6.94 us
    another operation x8, other arithmetic, pressure(): return jnp.cumsum(layer_mass, axis=0) - 0.5 * layer_mass  3.51 us
    unnamed x98, local copies, waits for them, and re-layouts  3.45 us
    unnamed x4, other arithmetic  3.38 us
    ppermute x2, local copies, waits for them, and re-layouts, with_halo(): after = lax.ppermute(leading, axis, down)  3.37 us
    slice x3, local copies, waits for them, and re-layouts, with_halo(): last = lax.slice_in_dim(value, length - width, length, axis=dim)  3.14 us
  transfers between devices with their start and end apart: 8, of which 0 were waited for; matrix products, arithmetic and copies ran while one was open for 15% of the time, Pallas kernels for 0%

commit v1 on v0

v1 whole, which is shorter than its diff:
```python
import functools

import jax
import jax.numpy as jnp
from jax import lax
from jax.experimental import pallas as pl
from jax.experimental.pallas import tpu as pltpu
from jax.sharding import PartitionSpec as P

MESH = pl.DeviceIdType.MESH
TIME_STEP = 0.25
EXPANSION = 0.2
CONTRACTION = 0.8
BOTTOM_DRAG = 1.0
LEVELS = 4
ENTRIES = 28
WET = 4
PAD = 8


def coefficients(w, we, ww, wn, ws, metrics, inv_h2):
    floor, zs, ms, rot, eddy = metrics[:5]
    mix = metrics[5:]
    rz, rm = 1.0 / zs, 1.0 / ms
    kx, ky = eddy * rz * rz, eddy * rm * rm
    hx, hy = 0.5 * rz, 0.5 * rm
    out = []
    for k in range(LEVELS):
        dtw = TIME_STEP * w[k]
        ax, ay = dtw * kx, dtw * ky
        ae, aw, an, as_ = ax * we[k], ax * ww[k], ay * wn[k], ay * ws[k]
        centre = 1.0 - (ae + aw) - (an + as_)
        t = dtw * inv_h2[k]
        below = above = None
        if k < LEVELS - 1:
            below = t * mix[k] * w[k + 1]
            centre = centre - below
        if k > 0:
            above = t * mix[k - 1] * w[k - 1]
            centre = centre - above
        drag = centre - jnp.where(floor == float(k), BOTTOM_DRAG * dtw, 0.0)
        out.append((ae, aw, an, as_, centre, drag, dtw * hx, dtw * hy, dtw * rot, below, above))
    return out


def advance(f, east, west, north, south, coef, heights):
    new = [[None] * LEVELS for _ in range(4)]
    sum_x = sum_y = None
    for k in range(LEVELS):
        ae, aw, an, as_, centre, drag, bx, by, rot, below, above = coef[k]
        u, v = f[2][k], f[3][k]
        bu, bv = bx * u, by * v
        ce, cw, cn, cs = ae - bu, aw + bu, an - bv, as_ + bv
        layer_x = (CONTRACTION * (east[1][k] - west[1][k]) - EXPANSION * (east[0][k] - west[0][k])) * heights[k]
        layer_y = (CONTRACTION * (north[1][k] - south[1][k]) - EXPANSION * (north[0][k] - south[0][k])) * heights[k]
        sum_x = layer_x if sum_x is None else sum_x + layer_x
        sum_y = layer_y if sum_y is None else sum_y + layer_y
        for c in range(4):
            val = ((centre if c < 2 else drag) * f[c][k] + (ce * east[c][k] + cw * west[c][k])
                   + (cn * north[c][k] + cs * south[c][k]))
            if below is not None:
                val = val + below * f[c][k + 1]
            if above is not None:
                val = val + above * f[c][k - 1]
            if c == 2:
                val = val + rot * v - bx * (sum_x - 0.5 * layer_x)
            if c == 3:
                val = val - rot * u - by * (sum_y - 0.5 * layer_y)
            new[c][k] = val
    return new


def kernel(nlon, nlat, rows, cols, *refs):
    ins, h_ref = refs[:11], refs[11]
    outs = refs[12:16]
    (x4, wet_i, floor_i, met, mix, x, y, coef_s, pack, ext, send_r, recv_r, corner, slab_c, slab_r, z,
     in_sem, out_sem, s_sem, r_sem) = refs[16:]
    lon, lat = lax.axis_index("lon"), lax.axis_index("lat")
    top, bottom = lat == nlat - 1, lat == 0
    f32 = jnp.float32

    loads = [pltpu.make_async_copy(ins[c], x4.at[c], in_sem.at[c]) for c in range(4)]
    loads.append(pltpu.make_async_copy(ins[4], wet_i, in_sem.at[4]))
    loads.append(pltpu.make_async_copy(ins[5], floor_i, in_sem.at[5]))
    loads += [pltpu.make_async_copy(ins[6 + m], met.at[m], in_sem.at[6 + m]) for m in range(4)]
    loads.append(pltpu.make_async_copy(ins[10], mix, in_sem.at[10]))
    for load in loads:
        load.start()

    e_lon, w_lon = lax.rem(lon + 1, nlon), lax.rem(lon + nlon - 1, nlon)
    n_lat = jnp.where(top, lat, lat + 1)
    n_lon = jnp.where(top, nlon - 1 - lon, lon)
    ne_lon = jnp.where(top, lax.rem(2 * nlon - 2 - lon, nlon), e_lon)
    nw_lon = jnp.where(top, lax.rem(nlon - lon, nlon), w_lon)
    s_lat = jnp.maximum(lat - 1, 0)
    ne_self = jnp.logical_and(top, ne_lon == lon)
    nw_self = jnp.logical_and(top, nw_lon == lon)
    ne_other = jnp.logical_not(ne_self)
    nw_other = jnp.logical_not(nw_self)
    inner = jnp.logical_not(bottom)

    for side in range(2):
        ext[side, rows:, :] = jnp.zeros((128 - rows, 128), f32)

    @pl.when(bottom)
    def _():
        recv_r[1, : 2 * 5 * LEVELS, :] = jnp.zeros((2 * 5 * LEVELS, cols), f32)
        recv_r[1, 2 * 5 * LEVELS :, :] = jnp.ones((2 * ENTRIES - 10 * LEVELS, cols), f32)

    barrier = pltpu.get_barrier_semaphore()

    def greet(dev):
        pl.semaphore_signal(barrier, inc=1, device_id=dev, device_id_type=MESH)

    greet((e_lon, lat))
    greet((w_lon, lat))
    greet((n_lon, n_lat))

    @pl.when(ne_other)
    def _():
        greet((ne_lon, n_lat))

    @pl.when(nw_other)
    def _():
        greet((nw_lon, n_lat))

    @pl.when(inner)
    def _():
        greet((lon, s_lat))
        greet((e_lon, s_lat))
        greet((w_lon, s_lat))

    lane = lax.broadcasted_iota(jnp.int32, (8, 128), 1)
    sub = lax.broadcasted_iota(jnp.int32, (8, 128), 0)
    heights = [jnp.full((8, 128), h_ref[k], f32) for k in range(LEVELS)]
    inv_h2 = [1.0 / (h * h) for h in heights]

    for load in loads:
        load.wait()

    chunks = rows // 8
    mets = [None, met.at[0], met.at[1], met.at[2], met.at[3], mix.at[0], mix.at[1], mix.at[2]]

    def metric(m, span):
        return floor_i[span, :].astype(f32) if m == 0 else mets[m][span, :]

    for r in range(chunks):
        span = pl.ds(8 * r, 8)
        held = pl.ds(PAD + 8 * r, 8)
        packed = jnp.zeros((8, 128), f32)
        wet = [wet_i[k, span, :].astype(f32) for k in range(LEVELS)]
        for c in range(ENTRIES):
            ch, k = c // LEVELS, c % LEVELS
            if ch < 4:
                val = x4[ch, k, span, :] * wet[k]
            elif ch == WET:
                val = wet[k]
            else:
                val = metric(c - 5 * LEVELS, span)
            if ch <= WET:
                x[ch, k, held, :] = val
            packed = jnp.where(lane // 4 == c, pltpu.roll(val, (4 * c + 2) % 128, 1), packed)
        pack[span, :] = packed

    def own_rows(c, first):
        ch, k = c // LEVELS, c % LEVELS
        if ch <= WET:
            return x[ch, k, pl.ds(PAD + first, 2), :]
        return metric(c - 5 * LEVELS, pl.ds(first, 2))

    for c in range(ENTRIES):
        low, high = own_rows(c, 0), own_rows(c, rows - 2)
        send_r[1, pl.ds(2 * c, 2), :] = low
        send_r[0, pl.ds(2 * c, 2), :] = high
        slab_r[c, 0:2, :] = high
        slab_r[c, 6:8, :] = low

    @pl.when(top)
    def _():
        for t in range(2 * ENTRIES // 8):
            val = send_r[0, pl.ds(8 * t, 8), :]
            val = jnp.where(sub % 2 == 1, pltpu.roll(val, 1, 0), pltpu.roll(val, 7, 0))
            step = 1
            while step < cols:
                val = jnp.where((lane // step) % 2 == 1, pltpu.roll(val, step, 1), pltpu.roll(val, cols - step, 1))
                step *= 2
            if 16 * LEVELS // 4 <= 8 * t < 32 * LEVELS // 4:
                val = -val
            send_r[0, pl.ds(8 * t, 8), :] = val

    last = pack[pl.ds(rows - 8, 8), :]
    turned = jnp.broadcast_to(last[7:8, :], (8, 128))
    for step in (1, 2):
        turned = jnp.where((lane // step) % 2 == 1, pltpu.roll(turned, step, 1), pltpu.roll(turned, 128 - step, 1))
    turned = jnp.where(jnp.logical_and(lane >= 8 * LEVELS, lane < 16 * LEVELS), -turned, turned)
    top_v = jnp.full((8, 128), top.astype(jnp.int32)) == 1
    folded = jnp.where(top_v, turned, last)
    corner[...] = folded

    @pl.when(ne_self)
    def _():
        ext[0, pl.ds(rows, 8), :] = folded

    @pl.when(nw_self)
    def _():
        ext[1, pl.ds(rows, 8), :] = folded

    pl.semaphore_wait(
        barrier,
        3 + ne_other.astype(jnp.int32) + nw_other.astype(jnp.int32) + 3 * inner.astype(jnp.int32),
    )

    def copy(src, dst, s, r, dev):
        return pltpu.make_async_remote_copy(
            src_ref=src, dst_ref=dst, send_sem=s_sem.at[s], recv_sem=r_sem.at[r], device_id=dev, device_id_type=MESH
        )

    body, up, down = pl.ds(0, rows), pl.ds(rows, 8), pl.ds(120, 8)
    to_east = copy(pack, ext.at[1, body], 0, 1, (e_lon, lat))
    to_west = copy(pack, ext.at[0, body], 1, 0, (w_lon, lat))
    fold_n = copy(send_r.at[0], recv_r.at[0], 2, 2, (n_lon, n_lat))
    fold_ne = copy(corner, ext.at[0, up], 4, 4, (ne_lon, n_lat))
    fold_nw = copy(corner, ext.at[1, up], 5, 5, (nw_lon, n_lat))
    to_n = copy(send_r.at[0], recv_r.at[1], 2, 3, (n_lon, n_lat))
    to_ne = copy(corner, ext.at[1, down], 4, 7, (ne_lon, n_lat))
    to_nw = copy(corner, ext.at[0, down], 5, 6, (nw_lon, n_lat))
    to_s = copy(send_r.at[1], recv_r.at[0], 3, 2, (lon, s_lat))
    to_se = copy(pack.at[pl.ds(0, 8)], ext.at[1, up], 6, 5, (e_lon, s_lat))
    to_sw = copy(pack.at[pl.ds(0, 8)], ext.at[0, up], 7, 4, (w_lon, s_lat))

    @pl.when(top)
    def _():
        fold_n.start()

    to_east.start()
    to_west.start()

    @pl.when(jnp.logical_and(top, ne_other))
    def _():
        fold_ne.start()

    @pl.when(jnp.logical_and(top, nw_other))
    def _():
        fold_nw.start()

    @pl.when(jnp.logical_not(top))
    def _():
        to_n.start()
        to_ne.start()
        to_nw.start()

    @pl.when(inner)
    def _():
        to_s.start()
        to_se.start()
        to_sw.start()

    to_s.wait_recv()

    @pl.when(inner)
    def _():
        to_n.wait_recv()
        to_ne.wait_recv()
        to_nw.wait_recv()

    @pl.when(ne_other)
    def _():
        to_sw.wait_recv()

    @pl.when(nw_other)
    def _():
        to_se.wait_recv()

    to_west.wait_recv()
    to_east.wait_recv()

    first_half = lane % 4 < 2
    for c in range(5 * LEVELS):
        ch, k = c // LEVELS, c % LEVELS
        x[ch, k, pl.ds(PAD + rows, 1), :] = recv_r[0, pl.ds(2 * c, 1), :]
        x[ch, k, pl.ds(PAD - 1, 1), :] = recv_r[1, pl.ds(2 * c + 1, 1), :]
    for c in range(ENTRIES):
        slab_r[c, 2:4, :] = recv_r[0, pl.ds(2 * c, 2), :]
        slab_r[c, 4:6, :] = recv_r[1, pl.ds(2 * c, 2), :]

    def side_of(hold, c, val):
        ends = pltpu.roll(hold, (128 - (4 * c + 2)) % 128, 1)
        east = pltpu.roll(jnp.where(lane == 0, ends, val), 127, 1)
        west = pltpu.roll(jnp.where(lane == 127, ends, val), 1, 1)
        return east, west

    def grid_of(fn):
        return [[fn(ch, k) for k in range(LEVELS)] for ch in range(5)]

    filler = jnp.zeros((128 - rows, 128), f32)
    own = jnp.concatenate([pack[...], filler], axis=0)
    half = lax.broadcasted_iota(jnp.int32, (128, 128), 1) % 4 < 2
    east_t = jnp.transpose(jnp.where(half, own, ext[0]))
    west_t = jnp.transpose(jnp.where(half, ext[1], own))
    for c in range(ENTRIES):
        slab_c[c, 0:4, :] = east_t[4 * c : 4 * c + 4, :]
        slab_c[c, 4:8, :] = west_t[4 * c : 4 * c + 4, :]

    def slab_step(slab, shifts):
        f = grid_of(lambda ch, k: slab[ch * LEVELS + k])
        e, w, n, s = shifts(f)
        metrics = [slab[5 * LEVELS + m] for m in range(8)]
        cf = coefficients(f[WET], e[WET], w[WET], n[WET], s[WET], metrics, inv_h2)
        return advance(f, e, w, n, s, cf, heights)

    def each(f, fn):
        return [[fn(ch, k, f[ch][k]) for k in range(LEVELS)] for ch in range(5)]

    def shifts_c(f):
        return (
            each(f, lambda ch, k, a: pltpu.roll(a, 7, 0)),
            each(f, lambda ch, k, a: pltpu.roll(a, 1, 0)),
            each(f, lambda ch, k, a: pltpu.roll(a, 127, 1)),
            each(f, lambda ch, k, a: pltpu.roll(a, 1, 1)),
        )

    z[...] = jnp.zeros((128, 128), f32)
    new = slab_step(slab_c, shifts_c)
    for c in range(4 * LEVELS):
        val = new[c // LEVELS][c % LEVELS]
        z[pl.ds(4 * c + 1, 1), :] = val[5:6, :]
        z[pl.ds(4 * c + 2, 1), :] = val[2:3, :]
    z[...] = jnp.transpose(z[...])

    is_east = lane % 4 == 2
    far_n = jnp.where(is_east, ext[0, up, :], ext[1, up, :])[0:1, :]
    far_s = jnp.where(is_east, ext[0, down, :], ext[1, down, :])[7:8, :]
    far = jnp.where(sub == 2, jnp.broadcast_to(far_n, (8, 128)), jnp.broadcast_to(far_s, (8, 128)))

    def shifts_r(f):
        pairs = each(f, lambda ch, k, a: side_of(far, ch * LEVELS + k, a))
        return (
            [[p[0] for p in line] for line in pairs],
            [[p[1] for p in line] for line in pairs],
            each(f, lambda ch, k, a: pltpu.roll(a, 7, 0)),
            each(f, lambda ch, k, a: pltpu.roll(a, 1, 0)),
        )

    new = slab_step(slab_r, shifts_r)
    for c in range(4 * LEVELS):
        val = new[c // LEVELS][c % LEVELS]
        y[c // LEVELS, c % LEVELS, pl.ds(PAD + rows, 1), :] = val[2:3, :]
        y[c // LEVELS, c % LEVELS, pl.ds(PAD - 1, 1), :] = val[5:6, :]

    def main_step(src, r, hold, channels):
        pick = lambda shift: [
            [src[ch, k, pl.ds(PAD + 8 * r + shift, 8), :] for k in range(LEVELS)] for ch in range(channels)
        ]
        f = pick(0)
        pairs = [[side_of(hold, ch * LEVELS + k, f[ch][k]) for k in range(LEVELS)] for ch in range(channels)]
        return (
            f,
            [[p[0] for p in line] for line in pairs],
            [[p[1] for p in line] for line in pairs],
            pick(1),
            pick(-1),
        )

    for r in range(chunks):
        span = pl.ds(8 * r, 8)
        hold = jnp.where(is_east, ext[0, span, :], ext[1, span, :])
        f, e, w, n, s = main_step(x, r, hold, 5)
        metrics = [metric(m, span) for m in range(8)]
        cf = coefficients(f[WET], e[WET], w[WET], n[WET], s[WET], metrics, inv_h2)
        new = advance(f, e, w, n, s, cf, heights)
        for k in range(LEVELS):
            for i, val in enumerate(cf[k]):
                if val is not None:
                    coef_s[i, k, span, :] = val
            for ch in range(4):
                y[ch, k, pl.ds(PAD + 8 * r, 8), :] = new[ch][k]

    for r in range(chunks):
        span = pl.ds(8 * r, 8)
        f, e, w, n, s = main_step(y, r, z[span, :], 4)
        cf = []
        for k in range(LEVELS):
            absent = {9} if k == LEVELS - 1 else ({10} if k == 0 else set())
            cf.append(tuple(None if i in absent else coef_s[i, k, span, :] for i in range(11)))
        new = advance(f, e, w, n, s, cf, heights)
        for ch in range(4):
            for k in range(LEVELS):
                x4[ch, k, span, :] = new[ch][k]

    stores = [pltpu.make_async_copy(x4.at[c], outs[c], out_sem.at[c]) for c in range(4)]
    for store in stores:
        store.start()

    to_east.wait_send()
    to_west.wait_send()
    to_n.wait_send()

    @pl.when(ne_other)
    def _():
        to_ne.wait_send()

    @pl.when(nw_other)
    def _():
        to_nw.wait_send()

    @pl.when(inner)
    def _():
        to_s.wait_send()
        to_se.wait_send()
        to_sw.wait_send()

    for store in stores:
        store.wait()


def solution(mesh):
    nlon, nlat = mesh.shape["lon"], mesh.shape["lat"]

    def shards(*args):
        levels, rows, cols = args[0].shape
        f32 = jnp.float32
        vmem = pltpu.VMEM
        return tuple(pl.pallas_call(
            functools.partial(kernel, nlon, nlat, rows, cols),
            out_shape=[jax.ShapeDtypeStruct((levels, rows, cols), f32)] * 4,
            in_specs=[pl.BlockSpec(memory_space=pl.ANY)] * 11 + [pl.BlockSpec(memory_space=pltpu.SMEM)],
            out_specs=[pl.BlockSpec(memory_space=pl.ANY)] * 4,
            scratch_shapes=[
                vmem((4, levels, rows, cols), f32),
                vmem((levels, rows, cols), jnp.int32),
                vmem((rows, cols), jnp.int32),
                vmem((4, rows, cols), f32),
                vmem((levels - 1, rows, cols), f32),
                vmem((5, levels, rows + 2 * PAD, cols), f32),
                vmem((4, levels, rows + 2 * PAD, cols), f32),
                vmem((11, levels, rows, cols), f32),
                vmem((rows, 128), f32),
                vmem((2, 128, 128), f32),
                vmem((2, 2 * ENTRIES, cols), f32),
                vmem((2, 2 * ENTRIES, cols), f32),
                vmem((8, 128), f32),
                vmem((ENTRIES, 8, 128), f32),
                vmem((ENTRIES, 8, cols), f32),
                vmem((128, 128), f32),
                pltpu.SemaphoreType.DMA((11,)),
                pltpu.SemaphoreType.DMA((4,)),
                pltpu.SemaphoreType.DMA((8,)),
                pltpu.SemaphoreType.DMA((8,)),
            ],
            compiler_params=pltpu.CompilerParams(
                collective_id=0, has_side_effects=True, vmem_limit_bytes=32 * 1024 * 1024
            ),
        )(*args))

    field, plane = P(None, "lat", "lon"), P("lat", "lon")
    return jax.shard_map(
        shards,
        mesh=mesh,
        in_specs=(field,) * 5 + (plane,) * 5 + (field, P()),
        out_specs=(field,) * 4,
        check_vma=False,
    )
```

time: 140 us -> 58.5 us (0.42)
  blocking collectives: 80.8 us -> 0 us
  Pallas kernels: 0 us -> 44.4 us
  starting transfers between devices: 20.1 us -> 0 us
  other arithmetic: 18.5 us -> 0 us
  local copies, waits for them, and re-layouts: 17.8 us -> 12.9 us
    all_gather x2 -> x0, blocking collectives: 80.8 us -> none  [fold_ghost(): gathered = lax.all_gather(top_row, 'lon', axis=2, tiled=True)]
    pallas_call x0 -> x1, Pallas kernels: none -> 44.4 us  [shards(): pl.pallas_call(functools.partial(kernel, nlon, nlat, rows, cols), out_sha...]
    ppermute x8 -> x0, starting transfers between devices: 20.1 us -> none  [the longest x4 13.1 us: with_halo(): after = lax.ppermute(leading, axis, down)]
    unnamed x98 -> x28, local copies, waits for them, and re-layouts: 3.45 us -> 12.9 us
    slice x9 -> x0, local copies, waits for them, and re-layouts: 6.38 us -> none  [the longest x3 3.14 us: with_halo(): last = lax.slice_in_dim(value, length - width, length, axis=dim)]
    ppermute x4 -> x0, local copies, waits for them, and re-layouts: 4.78 us -> none  [the longest x2 3.37 us: with_halo(): after = lax.ppermute(leading, axis, down)]
    mul x8 -> x0, other arithmetic: 4.37 us -> none  [the longest x3 1.83 us: mix_vertically(): diapycnal_diffusivity * (water_share[1:] * water_share[:-1]) * contrast]
    another operation x11 -> x0, other arithmetic: 3.61 us -> none  [the longest x8 3.51 us: pressure(): return jnp.cumsum(layer_mass, axis=0) - 0.5 * layer_mass]
  transfers between devices with their start and end apart: 8 -> 0, of which waited for: 0 -> 0; matrix products, arithmetic and copies ran while one was open for 15% -> 0% of each run, Pallas kernels for 0% -> 0%
where the time goes in v1:
time: 58.5 us; the launch traced here: 57.9 us
  Pallas kernels  44.4 us (76%)
  local copies, waits for them, and re-layouts  12.9 us (22%)
  between operations  0.67 us (1%)
    pallas_call x1, Pallas kernels, shards(): pl.pallas_call(functools.partial(kernel, nlon, nlat, rows, cols), out_sha...  44.4 us
    unnamed x28, local copies, waits for them, and re-layouts  12.9 us

profile of v1, /device:TPU:0, one launch (start us, length us, event | category | flops | bytes accessed | tf_op | source)
XLA Modules:
  0.0 57.9 jit_solution(5088236303469021770)
XLA Ops:
  0.6 0.0 copy-start
  0.6 0.9 %copy-done = f32[4,96,128]{2,1,0:T(8,128)S(1)} copy-done((f32[4,96,128]{2,1,0:T(8,128)S(1)}, f32[4,96,128]{2,1,0:T(8,128)}, u32[]{:S(2)}) %copy-start) | copy-done | bytes 196632
  1.6 0.9 %copy-done.1 = f32[4,96,128]{2,1,0:T(8,128)S(1)} copy-done((f32[4,96,128]{2,1,0:T(8,128)S(1)}, f32[4,96,128]{2,1,0:T(8,128)}, u32[]{:S(2)}) %copy-start.1) | copy-done | bytes 196632
  2.5 0.0 copy-start.2
  2.5 0.9 %copy-done.2 = f32[4,96,128]{2,1,0:T(8,128)S(1)} copy-done((f32[4,96,128]{2,1,0:T(8,128)S(1)}, f32[4,96,128]{2,1,0:T(8,128)}, u32[]{:S(2)}) %copy-start.2) | copy-done | bytes 196632
  3.4 0.0 copy-start.3
  3.4 0.9 %copy-done.3 = f32[4,96,128]{2,1,0:T(8,128)S(1)} copy-done((f32[4,96,128]{2,1,0:T(8,128)S(1)}, f32[4,96,128]{2,1,0:T(8,128)}, u32[]{:S(2)}) %copy-start.3) | copy-done | bytes 196632
  4.3 0.0 copy-start.4
  4.3 0.9 %copy-done.4 = s32[4,96,128]{2,1,0:T(8,128)S(1)} copy-done((s32[4,96,128]{2,1,0:T(8,128)S(1)}, s32[4,96,128]{2,1,0:T(8,128)}, u32[]{:S(2)}) %copy-start.4) | copy-done | bytes 196632
  5.3 0.0 copy-start.5
  5.3 0.9 %copy-done.5 = f32[3,96,128]{2,1,0:T(8,128)S(1)} copy-done((f32[3,96,128]{2,1,0:T(8,128)S(1)}, f32[3,96,128]{2,1,0:T(8,128)}, u32[]{:S(2)}) %copy-start.5) | copy-done | bytes 147480
  6.2 0.8 %copy-done.6 = s32[96,128]{1,0:T(8,128)S(1)} copy-done((s32[96,128]{1,0:T(8,128)S(1)}, s32[96,128]{1,0:T(8,128)}, u32[]{:S(2)}) %copy-start.6) | copy-done | bytes 49176
  7.0 0.0 copy-start.7
  7.0 0.8 %copy-done.7 = f32[96,128]{1,0:T(8,128)S(1)} copy-done((f32[96,128]{1,0:T(8,128)S(1)}, f32[96,128]{1,0:T(8,128)}, u32[]{:S(2)}) %copy-start.7) | copy-done | bytes 49176
  7.8 0.0 copy-start.8
  7.8 0.8 %copy-done.8 = f32[96,128]{1,0:T(8,128)S(1)} copy-done((f32[96,128]{1,0:T(8,128)S(1)}, f32[96,128]{1,0:T(8,128)}, u32[]{:S(2)}) %copy-start.8) | copy-done | bytes 49176
  8.6 0.8 %copy-done.9 = f32[96,128]{1,0:T(8,128)S(1)} copy-done((f32[96,128]{1,0:T(8,128)S(1)}, f32[96,128]{1,0:T(8,128)}, u32[]{:S(2)}) %copy-start.9) | copy-done | bytes 49176
  9.4 0.8 %copy-done.10 = f32[96,128]{1,0:T(8,128)S(1)} copy-done((f32[96,128]{1,0:T(8,128)S(1)}, f32[96,128]{1,0:T(8,128)}, u32[]{:S(2)}) %copy-start.10) | copy-done | bytes 49176
  10.2 0.7 %copy-done.11 = f32[4]{0:T(128)S(1)} copy-done((f32[4]{0:T(128)S(1)}, f32[4]{0:T(128)}, u32[]{:S(2)}) %copy-start.11) | copy-done | bytes 40
  10.8 44.4 %shard_map.147 = (f32[4,96,128]{2,1,0:T(8,128)S(1)}, f32[4,96,128]{2,1,0:T(8,128)S(1)}, f32[4,96,128]{2,1,0:T(8,128)S(1)}, f32[4,96,128]{2,1,0:T(8,128)S(1)}) custom-call(f32[4,96,128]{2,1,0:T(8,128)S(1)} %copy-done, f32[4,96,128]{2,1,0:T(8,128)S(1)} %copy-done.1, f32[4,96,128]{2,1,0:T(8,128)S(1)} %copy-done.2, f32[4,96,128]{2,1,0:T(8,128)S(1)} %copy-done.3, ...), custom_call_target="tpu_custom_call" | custom-call | tf_op jit(solution)/shard_map/pallas_call | solution.py:423
  55.2 0.7 %copy.20 = f32[4,96,128]{2,1,0:T(8,128)} copy(f32[4,96,128]{2,1,0:T(8,128)S(1)} %get-tuple-element.8) | data formatting | bytes 393216
  55.9 0.7 %copy.21 = f32[4,96,128]{2,1,0:T(8,128)} copy(f32[4,96,128]{2,1,0:T(8,128)S(1)} %get-tuple-element.9) | data formatting | bytes 393216
  56.6 0.7 %copy.22 = f32[4,96,128]{2,1,0:T(8,128)} copy(f32[4,96,128]{2,1,0:T(8,128)S(1)} %get-tuple-element.10) | data formatting | bytes 393216
  57.2 0.7 %copy.23 = f32[4,96,128]{2,1,0:T(8,128)} copy(f32[4,96,128]{2,1,0:T(8,128)S(1)} %get-tuple-element.11) | data formatting | bytes 393216
  (5 shorter events, 0.0 us)
Async XLA Ops:
  0.6 0.9 %copy-start = (f32[4,96,128]{2,1,0:T(8,128)S(1)}, f32[4,96,128]{2,1,0:T(8,128)}, u32[]{:S(2)}) copy-start(f32[4,96,128]{2,1,0:T(8,128)} %refs_0_.1) | copy-start | bytes 589828
  1.6 0.9 %copy-start.1 = (f32[4,96,128]{2,1,0:T(8,128)S(1)}, f32[4,96,128]{2,1,0:T(8,128)}, u32[]{:S(2)}) copy-start(f32[4,96,128]{2,1,0:T(8,128)} %refs_1_.1) | copy-start | bytes 589828
  2.5 0.9 %copy-start.2 = (f32[4,96,128]{2,1,0:T(8,128)S(1)}, f32[4,96,128]{2,1,0:T(8,128)}, u32[]{:S(2)}) copy-start(f32[4,96,128]{2,1,0:T(8,128)} %refs_2_.1) | copy-start | bytes 589828
  3.4 0.9 %copy-start.3 = (f32[4,96,128]{2,1,0:T(8,128)S(1)}, f32[4,96,128]{2,1,0:T(8,128)}, u32[]{:S(2)}) copy-start(f32[4,96,128]{2,1,0:T(8,128)} %refs_3_.1) | copy-start | bytes 589828
  4.3 0.9 %copy-start.4 = (s32[4,96,128]{2,1,0:T(8,128)S(1)}, s32[4,96,128]{2,1,0:T(8,128)}, u32[]{:S(2)}) copy-start(s32[4,96,128]{2,1,0:T(8,128)} %refs_4_.1) | copy-start | bytes 589828
  5.3 0.9 %copy-start.5 = (f32[3,96,128]{2,1,0:T(8,128)S(1)}, f32[3,96,128]{2,1,0:T(8,128)}, u32[]{:S(2)}) copy-start(f32[3,96,128]{2,1,0:T(8,128)} %refs_10_.1) | copy-start | bytes 442372
  6.2 0.8 %copy-start.6 = (s32[96,128]{1,0:T(8,128)S(1)}, s32[96,128]{1,0:T(8,128)}, u32[]{:S(2)}) copy-start(s32[96,128]{1,0:T(8,128)} %refs_5_.1) | copy-start | bytes 147460
  7.0 0.8 %copy-start.7 = (f32[96,128]{1,0:T(8,128)S(1)}, f32[96,128]{1,0:T(8,128)}, u32[]{:S(2)}) copy-start(f32[96,128]{1,0:T(8,128)} %refs_6_.1) | copy-start | bytes 147460
  7.8 0.8 %copy-start.8 = (f32[96,128]{1,0:T(8,128)S(1)}, f32[96,128]{1,0:T(8,128)}, u32[]{:S(2)}) copy-start(f32[96,128]{1,0:T(8,128)} %refs_7_.1) | copy-start | bytes 147460
  8.6 0.8 %copy-start.9 = (f32[96,128]{1,0:T(8,128)S(1)}, f32[96,128]{1,0:T(8,128)}, u32[]{:S(2)}) copy-start(f32[96,128]{1,0:T(8,128)} %refs_8_.1) | copy-start | bytes 147460
  9.4 0.8 %copy-start.10 = (f32[96,128]{1,0:T(8,128)S(1)}, f32[96,128]{1,0:T(8,128)}, u32[]{:S(2)}) copy-start(f32[96,128]{1,0:T(8,128)} %refs_9_.1) | copy-start | bytes 147460
  10.2 0.7 %copy-start.11 = (f32[4]{0:T(128)S(1)}, f32[4]{0:T(128)}, u32[]{:S(2)}) copy-start(f32[4]{0:T(128)} %refs_11_.1) | copy-start | bytes 52

commit v2 on v1

--- a/solution.py
+++ b/solution.py
@@ -18,56 +18,48 @@
 PAD = 8
 
 
-def coefficients(w, we, ww, wn, ws, metrics, inv_h2):
+def level_coefficients(k, w, we, ww, wn, ws, metrics, inv_h2, w_below, w_above):
     floor, zs, ms, rot, eddy = metrics[:5]
     mix = metrics[5:]
     rz, rm = 1.0 / zs, 1.0 / ms
-    kx, ky = eddy * rz * rz, eddy * rm * rm
-    hx, hy = 0.5 * rz, 0.5 * rm
-    out = []
-    for k in range(LEVELS):
-        dtw = TIME_STEP * w[k]
-        ax, ay = dtw * kx, dtw * ky
-        ae, aw, an, as_ = ax * we[k], ax * ww[k], ay * wn[k], ay * ws[k]
-        centre = 1.0 - (ae + aw) - (an + as_)
-        t = dtw * inv_h2[k]
-        below = above = None
-        if k < LEVELS - 1:
-            below = t * mix[k] * w[k + 1]
-            centre = centre - below
-        if k > 0:
-            above = t * mix[k - 1] * w[k - 1]
-            centre = centre - above
-        drag = centre - jnp.where(floor == float(k), BOTTOM_DRAG * dtw, 0.0)
-        out.append((ae, aw, an, as_, centre, drag, dtw * hx, dtw * hy, dtw * rot, below, above))
-    return out
-
-
-def advance(f, east, west, north, south, coef, heights):
-    new = [[None] * LEVELS for _ in range(4)]
-    sum_x = sum_y = None
-    for k in range(LEVELS):
-        ae, aw, an, as_, centre, drag, bx, by, rot, below, above = coef[k]
-        u, v = f[2][k], f[3][k]
-        bu, bv = bx * u, by * v
-        ce, cw, cn, cs = ae - bu, aw + bu, an - bv, as_ + bv
-        layer_x = (CONTRACTION * (east[1][k] - west[1][k]) - EXPANSION * (east[0][k] - west[0][k])) * heights[k]
-        layer_y = (CONTRACTION * (north[1][k] - south[1][k]) - EXPANSION * (north[0][k] - south[0][k])) * heights[k]
-        sum_x = layer_x if sum_x is None else sum_x + layer_x
-        sum_y = layer_y if sum_y is None else sum_y + layer_y
-        for c in range(4):
-            val = ((centre if c < 2 else drag) * f[c][k] + (ce * east[c][k] + cw * west[c][k])
-                   + (cn * north[c][k] + cs * south[c][k]))
-            if below is not None:
-                val = val + below * f[c][k + 1]
-            if above is not None:
-                val = val + above * f[c][k - 1]
-            if c == 2:
-                val = val + rot * v - bx * (sum_x - 0.5 * layer_x)
-            if c == 3:
-                val = val - rot * u - by * (sum_y - 0.5 * layer_y)
-            new[c][k] = val
-    return new
+    dtw = TIME_STEP * w
+    ax, ay = dtw * (eddy * rz * rz), dtw * (eddy * rm * rm)
+    ae, aw, an, as_ = ax * we, ax * ww, ay * wn, ay * ws
+    centre = 1.0 - (ae + aw) - (an + as_)
+    t = dtw * inv_h2[k]
+    below = above = None
+    if k < LEVELS - 1:
+        below = t * mix[k] * w_below
+        centre = centre - below
+    if k > 0:
+        above = t * mix[k - 1] * w_above
+        centre = centre - above
+    drag = centre - jnp.where(floor == float(k), BOTTOM_DRAG * dtw, 0.0)
+    return ae, aw, an, as_, centre, drag, dtw * (0.5 * rz), dtw * (0.5 * rm), dtw * rot, below, above
+
+
+def advance_level(k, f, f_below, f_above, east, west, north, south, coef, heights, sums):
+    ae, aw, an, as_, centre, drag, bx, by, rot, below, above = coef
+    u, v = f[2], f[3]
+    bu, bv = bx * u, by * v
+    ce, cw, cn, cs = ae - bu, aw + bu, an - bv, as_ + bv
+    layer_x = (CONTRACTION * (east[1] - west[1]) - EXPANSION * (east[0] - west[0])) * heights[k]
+    layer_y = (CONTRACTION * (north[1] - south[1]) - EXPANSION * (north[0] - south[0])) * heights[k]
+    sum_x, sum_y = (layer_x, layer_y) if k == 0 else (sums[0] + layer_x, sums[1] + layer_y)
+    new = []
+    for c in range(4):
+        val = ((centre if c < 2 else drag) * f[c] + (ce * east[c] + cw * west[c])
+               + (cn * north[c] + cs * south[c]))
+        if below is not None:
+            val = val + below * f_below[c]
+        if above is not None:
+            val = val + above * f_above[c]
+        if c == 2:
+            val = val + rot * v - bx * (sum_x - 0.5 * layer_x)
+        if c == 3:
+            val = val - rot * u - by * (sum_y - 0.5 * layer_y)
+        new.append(val)
+    return new, (sum_x, sum_y)
 
 
 def kernel(nlon, nlat, rows, cols, *refs):
@@ -144,9 +136,12 @@
     def metric(m, span):
         return floor_i[span, :].astype(f32) if m == 0 else mets[m][span, :]
 
-    for r in range(chunks):
-        span = pl.ds(8 * r, 8)
-        held = pl.ds(PAD + 8 * r, 8)
+    group = lane >> 2
+
+    @pl.loop(0, chunks)
+    def _(r):
+        span = pl.ds(pl.multiple_of(8 * r, 8), 8)
+        held = pl.ds(pl.multiple_of(PAD + 8 * r, 8), 8)
         packed = jnp.zeros((8, 128), f32)
         wet = [wet_i[k, span, :].astype(f32) for k in range(LEVELS)]
         for c in range(ENTRIES):
@@ -159,7 +154,7 @@
                 val = metric(c - 5 * LEVELS, span)
             if ch <= WET:
                 x[ch, k, held, :] = val
-            packed = jnp.where(lane // 4 == c, pltpu.roll(val, (4 * c + 2) % 128, 1), packed)
+            packed = jnp.where(group == c, pltpu.roll(val, (4 * c + 2) % 128, 1), packed)
         pack[span, :] = packed
 
     def own_rows(c, first):
@@ -177,21 +172,22 @@
 
     @pl.when(top)
     def _():
-        for t in range(2 * ENTRIES // 8):
-            val = send_r[0, pl.ds(8 * t, 8), :]
-            val = jnp.where(sub % 2 == 1, pltpu.roll(val, 1, 0), pltpu.roll(val, 7, 0))
+        @pl.loop(0, 2 * ENTRIES // 8)
+        def _(t):
+            span = pl.ds(pl.multiple_of(8 * t, 8), 8)
+            val = send_r[0, span, :]
+            val = jnp.where((sub & 1) == 1, pltpu.roll(val, 1, 0), pltpu.roll(val, 7, 0))
             step = 1
             while step < cols:
-                val = jnp.where((lane // step) % 2 == 1, pltpu.roll(val, step, 1), pltpu.roll(val, cols - step, 1))
+                val = jnp.where((lane & step) != 0, pltpu.roll(val, step, 1), pltpu.roll(val, cols - step, 1))
                 step *= 2
-            if 16 * LEVELS // 4 <= 8 * t < 32 * LEVELS // 4:
-                val = -val
-            send_r[0, pl.ds(8 * t, 8), :] = val
+            flipped = jnp.logical_and(8 * t + sub >= 4 * LEVELS, 8 * t + sub < 8 * LEVELS)
+            send_r[0, span, :] = jnp.where(flipped, -val, val)
 
     last = pack[pl.ds(rows - 8, 8), :]
     turned = jnp.broadcast_to(last[7:8, :], (8, 128))
     for step in (1, 2):
-        turned = jnp.where((lane // step) % 2 == 1, pltpu.roll(turned, step, 1), pltpu.roll(turned, 128 - step, 1))
+        turned = jnp.where((lane & step) != 0, pltpu.roll(turned, step, 1), pltpu.roll(turned, 128 - step, 1))
     turned = jnp.where(jnp.logical_and(lane >= 8 * LEVELS, lane < 16 * LEVELS), -turned, turned)
     top_v = jnp.full((8, 128), top.astype(jnp.int32)) == 1
     folded = jnp.where(top_v, turned, last)
@@ -274,7 +270,6 @@
     to_west.wait_recv()
     to_east.wait_recv()
 
-    first_half = lane % 4 < 2
     for c in range(5 * LEVELS):
         ch, k = c // LEVELS, c % LEVELS
         x[ch, k, pl.ds(PAD + rows, 1), :] = recv_r[0, pl.ds(2 * c, 1), :]
@@ -289,103 +284,98 @@
         west = pltpu.roll(jnp.where(lane == 127, ends, val), 1, 1)
         return east, west
 
-    def grid_of(fn):
-        return [[fn(ch, k) for k in range(LEVELS)] for ch in range(5)]
-
     filler = jnp.zeros((128 - rows, 128), f32)
     own = jnp.concatenate([pack[...], filler], axis=0)
-    half = lax.broadcasted_iota(jnp.int32, (128, 128), 1) % 4 < 2
+    half = (lax.broadcasted_iota(jnp.int32, (128, 128), 1) & 3) < 2
     east_t = jnp.transpose(jnp.where(half, own, ext[0]))
     west_t = jnp.transpose(jnp.where(half, ext[1], own))
     for c in range(ENTRIES):
         slab_c[c, 0:4, :] = east_t[4 * c : 4 * c + 4, :]
         slab_c[c, 4:8, :] = west_t[4 * c : 4 * c + 4, :]
 
-    def slab_step(slab, shifts):
-        f = grid_of(lambda ch, k: slab[ch * LEVELS + k])
-        e, w, n, s = shifts(f)
+    def slab_step(slab, east_west, north_south, keep):
         metrics = [slab[5 * LEVELS + m] for m in range(8)]
-        cf = coefficients(f[WET], e[WET], w[WET], n[WET], s[WET], metrics, inv_h2)
-        return advance(f, e, w, n, s, cf, heights)
-
-    def each(f, fn):
-        return [[fn(ch, k, f[ch][k]) for k in range(LEVELS)] for ch in range(5)]
-
-    def shifts_c(f):
-        return (
-            each(f, lambda ch, k, a: pltpu.roll(a, 7, 0)),
-            each(f, lambda ch, k, a: pltpu.roll(a, 1, 0)),
-            each(f, lambda ch, k, a: pltpu.roll(a, 127, 1)),
-            each(f, lambda ch, k, a: pltpu.roll(a, 1, 1)),
-        )
+        f = [[slab[ch * LEVELS + k] for k in range(LEVELS)] for ch in range(5)]
+        sums = None
+        for k in range(LEVELS):
+            now = [f[ch][k] for ch in range(5)]
+            lower = [f[ch][k + 1] for ch in range(5)] if k < LEVELS - 1 else [None] * 5
+            upper = [f[ch][k - 1] for ch in range(5)] if k > 0 else [None] * 5
+            e, w = zip(*[east_west(ch * LEVELS + k, now[ch]) for ch in range(5)])
+            n, s = zip(*[north_south(now[ch]) for ch in range(5)])
+            cf = level_coefficients(k, now[WET], e[WET], w[WET], n[WET], s[WET], metrics, inv_h2, lower[WET], upper[WET])
+            new, sums = advance_level(k, now, lower, upper, e, w, n, s, cf, heights, sums)
+            for ch in range(4):
+                keep(ch, k, new[ch])
+
+    def along_rows(a):
+        return pltpu.roll(a, 7, 0), pltpu.roll(a, 1, 0)
+
+    def along_lanes(a):
+        return pltpu.roll(a, 127, 1), pltpu.roll(a, 1, 1)
 
     z[...] = jnp.zeros((128, 128), f32)
-    new = slab_step(slab_c, shifts_c)
-    for c in range(4 * LEVELS):
-        val = new[c // LEVELS][c % LEVELS]
+
+    def keep_column(ch, k, val):
+        c = ch * LEVELS + k
         z[pl.ds(4 * c + 1, 1), :] = val[5:6, :]
         z[pl.ds(4 * c + 2, 1), :] = val[2:3, :]
+
+    slab_step(slab_c, lambda c, a: along_rows(a), along_lanes, keep_column)
     z[...] = jnp.transpose(z[...])
 
-    is_east = lane % 4 == 2
+    is_east = (lane & 3) == 2
     far_n = jnp.where(is_east, ext[0, up, :], ext[1, up, :])[0:1, :]
     far_s = jnp.where(is_east, ext[0, down, :], ext[1, down, :])[7:8, :]
     far = jnp.where(sub == 2, jnp.broadcast_to(far_n, (8, 128)), jnp.broadcast_to(far_s, (8, 128)))
 
-    def shifts_r(f):
-        pairs = each(f, lambda ch, k, a: side_of(far, ch * LEVELS + k, a))
-        return (
-            [[p[0] for p in line] for line in pairs],
-            [[p[1] for p in line] for line in pairs],
-            each(f, lambda ch, k, a: pltpu.roll(a, 7, 0)),
-            each(f, lambda ch, k, a: pltpu.roll(a, 1, 0)),
-        )
-
-    new = slab_step(slab_r, shifts_r)
-    for c in range(4 * LEVELS):
-        val = new[c // LEVELS][c % LEVELS]
-        y[c // LEVELS, c % LEVELS, pl.ds(PAD + rows, 1), :] = val[2:3, :]
-        y[c // LEVELS, c % LEVELS, pl.ds(PAD - 1, 1), :] = val[5:6, :]
-
-    def main_step(src, r, hold, channels):
-        pick = lambda shift: [
-            [src[ch, k, pl.ds(PAD + 8 * r + shift, 8), :] for k in range(LEVELS)] for ch in range(channels)
-        ]
-        f = pick(0)
-        pairs = [[side_of(hold, ch * LEVELS + k, f[ch][k]) for k in range(LEVELS)] for ch in range(channels)]
-        return (
-            f,
-            [[p[0] for p in line] for line in pairs],
-            [[p[1] for p in line] for line in pairs],
-            pick(1),
-            pick(-1),
-        )
-
-    for r in range(chunks):
-        span = pl.ds(8 * r, 8)
+    def keep_row(ch, k, val):
+        y[ch, k, pl.ds(PAD + rows, 1), :] = val[2:3, :]
+        y[ch, k, pl.ds(PAD - 1, 1), :] = val[5:6, :]
+
+    slab_step(slab_r, lambda c, a: side_of(far, c, a), along_rows, keep_row)
+
+    def neighbours(src, r, k, hold, channels):
+        def pick(ch, at, shift):
+            return src[ch, at, pl.ds(PAD + 8 * r + shift, 8), :]
+
+        now = [pick(ch, k, 0) for ch in range(channels)]
+        lower = [pick(ch, k + 1, 0) for ch in range(channels)] if k < LEVELS - 1 else [None] * 5
+        upper = [pick(ch, k - 1, 0) for ch in range(channels)] if k > 0 else [None] * 5
+        e, w = zip(*[side_of(hold, ch * LEVELS + k, now[ch]) for ch in range(channels)])
+        n = [pick(ch, k, 1) for ch in range(channels)]
+        s = [pick(ch, k, -1) for ch in range(channels)]
+        return now, lower, upper, e, w, n, s
+
+    @pl.loop(0, chunks)
+    def _(r):
+        span = pl.ds(pl.multiple_of(8 * r, 8), 8)
+        held = pl.ds(pl.multiple_of(PAD + 8 * r, 8), 8)
         hold = jnp.where(is_east, ext[0, span, :], ext[1, span, :])
-        f, e, w, n, s = main_step(x, r, hold, 5)
         metrics = [metric(m, span) for m in range(8)]
-        cf = coefficients(f[WET], e[WET], w[WET], n[WET], s[WET], metrics, inv_h2)
-        new = advance(f, e, w, n, s, cf, heights)
+        sums = None
         for k in range(LEVELS):
-            for i, val in enumerate(cf[k]):
+            now, lower, upper, e, w, n, s = neighbours(x, r, k, hold, 5)
+            cf = level_coefficients(k, now[WET], e[WET], w[WET], n[WET], s[WET], metrics, inv_h2, lower[WET], upper[WET])
+            new, sums = advance_level(k, now, lower, upper, e, w, n, s, cf, heights, sums)
+            for i, val in enumerate(cf):
                 if val is not None:
                     coef_s[i, k, span, :] = val
             for ch in range(4):
-                y[ch, k, pl.ds(PAD + 8 * r, 8), :] = new[ch][k]
-
-    for r in range(chunks):
-        span = pl.ds(8 * r, 8)
-        f, e, w, n, s = main_step(y, r, z[span, :], 4)
-        cf = []
+                y[ch, k, held, :] = new[ch]
+
+    @pl.loop(0, chunks)
+    def _(r):
+        span = pl.ds(pl.multiple_of(8 * r, 8), 8)
+        hold = z[span, :]
+        sums = None
         for k in range(LEVELS):
+            now, lower, upper, e, w, n, s = neighbours(y, r, k, hold, 4)
             absent = {9} if k == LEVELS - 1 else ({10} if k == 0 else set())
-            cf.append(tuple(None if i in absent else coef_s[i, k, span, :] for i in range(11)))
-        new = advance(f, e, w, n, s, cf, heights)
-        for ch in range(4):
-            for k in range(LEVELS):
-                x4[ch, k, span, :] = new[ch][k]
+            cf = [None if i in absent else coef_s[i, k, span, :] for i in range(11)]
+            new, sums = advance_level(k, now, lower, upper, e, w, n, s, cf, heights, sums)
+            for ch in range(4):
+                x4[ch, k, span, :] = new[ch]
 
     stores = [pltpu.make_async_copy(x4.at[c], outs[c], out_sem.at[c]) for c in range(4)]
     for store in stores:
@@ -423,8 +413,8 @@
         return tuple(pl.pallas_call(
             functools.partial(kernel, nlon, nlat, rows, cols),
             out_shape=[jax.ShapeDtypeStruct((levels, rows, cols), f32)] * 4,
-            in_specs=[pl.BlockSpec(memory_space=pl.ANY)] * 11 + [pl.BlockSpec(memory_space=pltpu.SMEM)],
-            out_specs=[pl.BlockSpec(memory_space=pl.ANY)] * 4,
+            in_specs=[pl.BlockSpec(memory_space=pltpu.HBM)] * 11 + [pl.BlockSpec(memory_space=pltpu.SMEM)],
+            out_specs=[pl.BlockSpec(memory_space=pltpu.HBM)] * 4,
             scratch_shapes=[
                 vmem((4, levels, rows, cols), f32),
                 vmem((levels, rows, cols), jnp.int32),
@@ -448,7 +438,7 @@
                 pltpu.SemaphoreType.DMA((8,)),
             ],
             compiler_params=pltpu.CompilerParams(
-                collective_id=0, has_side_effects=True, vmem_limit_bytes=32 * 1024 * 1024
+                collective_id=0, has_side_effects=True, vmem_limit_bytes=60 * 1024 * 1024
             ),
         )(*args))
 

time: 58.5 us -> 26.5 us (0.45)
  Pallas kernels: 44.4 us -> 21.3 us
  local copies, waits for them, and re-layouts: 12.9 us -> 4.33 us
    pallas_call x1, Pallas kernels: 44.4 us -> 21.3 us  [shards(): pl.pallas_call(functools.partial(kernel, nlon, nlat, rows, cols), out_sha...]
    unnamed x28 -> x10, local copies, waits for them, and re-layouts: 12.9 us -> 4.33 us
where the time goes in v2:
time: 26.5 us; the launch traced here: 26.3 us
  Pallas kernels  21.3 us (80%)
  local copies, waits for them, and re-layouts  4.33 us (16%)
  between operations  0.66 us (2%)
    pallas_call x1, Pallas kernels, shards(): pl.pallas_call(functools.partial(kernel, nlon, nlat, rows, cols), out_sha...  21.3 us
    unnamed x10, local copies, waits for them, and re-layouts  4.33 us

profile of v2, /device:TPU:0, one launch (start us, length us, event | category | flops | bytes accessed | tf_op | source)
XLA Modules:
  0.0 26.3 jit_solution(13449204709647892122)
XLA Ops:
  0.6 21.3 %shard_map.147 = (f32[4,96,128]{2,1,0:T(8,128)}, f32[4,96,128]{2,1,0:T(8,128)}, f32[4,96,128]{2,1,0:T(8,128)}, f32[4,96,128]{2,1,0:T(8,128)}) custom-call(f32[4,96,128]{2,1,0:T(8,128)} %refs_0_.1, f32[4,96,128]{2,1,0:T(8,128)} %refs_1_.1, f32[4,96,128]{2,1,0:T(8,128)} %refs_2_.1, f32[4,96,128]{2,1,0:T(8,128)} %refs_3_.1, s32[4,96,128]{2,1,0:T(8,128)} %refs_4_.1, ...), custom_call_target="tpu_custom_call" | custom-call | tf_op jit(solution)/shard_map/pallas_call | solution.py:413
  22.0 0.0 copy-start.2
  22.0 1.7 %copy.20 = f32[4,96,128]{2,1,0:T(8,128)} copy(f32[4,96,128]{2,1,0:T(8,128)} %get-tuple-element.8) | data formatting | bytes 393216
  23.6 0.0 copy-done.2
  23.6 0.0 copy-start.1
  23.6 0.7 %copy.21 = f32[4,96,128]{2,1,0:T(8,128)} copy(f32[4,96,128]{2,1,0:T(8,128)S(1)} %copy-done.2) | data formatting | bytes 393216
  24.3 0.3 %copy-done.1 = f32[4,96,128]{2,1,0:T(8,128)S(1)} copy-done((f32[4,96,128]{2,1,0:T(8,128)S(1)}, f32[4,96,128]{2,1,0:T(8,128)}, u32[]{:S(2)}) %copy-start.1) | copy-done | bytes 196632
  24.6 0.0 copy-start
  24.6 0.7 %copy.22 = f32[4,96,128]{2,1,0:T(8,128)} copy(f32[4,96,128]{2,1,0:T(8,128)S(1)} %copy-done.1) | data formatting | bytes 393216
  25.3 0.3 %copy-done = f32[4,96,128]{2,1,0:T(8,128)S(1)} copy-done((f32[4,96,128]{2,1,0:T(8,128)S(1)}, f32[4,96,128]{2,1,0:T(8,128)}, u32[]{:S(2)}) %copy-start) | copy-done | bytes 196632
  25.6 0.7 %copy.23 = f32[4,96,128]{2,1,0:T(8,128)} copy(f32[4,96,128]{2,1,0:T(8,128)S(1)} %copy-done) | data formatting | bytes 393216
Async XLA Ops:
  22.0 1.7 %copy-start.2 = (f32[4,96,128]{2,1,0:T(8,128)S(1)}, f32[4,96,128]{2,1,0:T(8,128)}, u32[]{:S(2)}) copy-start(f32[4,96,128]{2,1,0:T(8,128)} %get-tuple-element.9) | copy-start | bytes 589828
  23.6 1.0 %copy-start.1 = (f32[4,96,128]{2,1,0:T(8,128)S(1)}, f32[4,96,128]{2,1,0:T(8,128)}, u32[]{:S(2)}) copy-start(f32[4,96,128]{2,1,0:T(8,128)} %get-tuple-element.10) | copy-start | bytes 589828
  24.6 1.0 %copy-start = (f32[4,96,128]{2,1,0:T(8,128)S(1)}, f32[4,96,128]{2,1,0:T(8,128)}, u32[]{:S(2)}) copy-start(f32[4,96,128]{2,1,0:T(8,128)} %get-tuple-element.11) | copy-start | bytes 589828

commit v3 on v2

v3 whole, which is shorter than its diff:
```python
import functools

import jax
import jax.numpy as jnp
from jax import lax
from jax.experimental import pallas as pl
from jax.experimental.pallas import tpu as pltpu
from jax.sharding import PartitionSpec as P

MESH = pl.DeviceIdType.MESH
TIME_STEP = 0.25
EXPANSION = 0.2
CONTRACTION = 0.8
BOTTOM_DRAG = 1.0
LEVELS = 4
ENTRIES = 28
FIELDS = 16
WET = 4
PAD = 8


def placed(c):
    if 8 <= c < 12:
        return c + 4
    if 12 <= c < 16:
        return c - 4
    return {21: 22, 22: 21}.get(c, c)


def kernel(nlon, nlat, rows, cols, *refs):
    ins, h_ref = refs[:11], refs[11]
    outs = refs[12:16]
    (st, hold, wet_i, floor_i, pack, ext, send_r, recv_r, corner, z, in_sem, out_sem, s_sem, r_sem) = refs[16:]
    lon, lat = lax.axis_index("lon"), lax.axis_index("lat")
    top, bottom = lat == nlat - 1, lat == 0
    topi = top.astype(jnp.int32)
    f32 = jnp.float32
    chunks = rows // 8
    row_tile, col_tile = chunks, chunks + 1
    row0, col0 = PAD + 8 * (chunks + 1), PAD + 8 * (chunks + 2)
    body = pl.ds(PAD, rows)

    wet0, met0 = 2 * FIELDS, 2 * FIELDS + LEVELS
    loads = [pltpu.make_async_copy(ins[c], st.at[pl.ds(4 * c, 4), body], in_sem.at[c]) for c in range(4)]
    loads.append(pltpu.make_async_copy(ins[4], wet_i, in_sem.at[4]))
    loads.append(pltpu.make_async_copy(ins[5], floor_i, in_sem.at[5]))
    loads += [pltpu.make_async_copy(ins[6 + m], st.at[met0 + 1 + m, body], in_sem.at[6 + m]) for m in range(4)]
    loads.append(pltpu.make_async_copy(ins[10], st.at[pl.ds(met0 + 5, 3), body], in_sem.at[10]))
    for load in loads:
        load.start()

    e_lon, w_lon = lax.rem(lon + 1, nlon), lax.rem(lon + nlon - 1, nlon)
    n_lat = jnp.where(top, lat, lat + 1)
    n_lon = jnp.where(top, nlon - 1 - lon, lon)
    ne_lon = jnp.where(top, lax.rem(2 * nlon - 2 - lon, nlon), e_lon)
    nw_lon = jnp.where(top, lax.rem(nlon - lon, nlon), w_lon)
    s_lat = jnp.maximum(lat - 1, 0)
    ne_self = jnp.logical_and(top, ne_lon == lon)
    nw_self = jnp.logical_and(top, nw_lon == lon)
    ne_other = jnp.logical_not(ne_self)
    nw_other = jnp.logical_not(nw_self)
    inner = jnp.logical_not(bottom)

    @pl.when(bottom)
    def _():
        ext[0, 120:, :] = jnp.zeros((8, 128), f32)
        ext[1, 120:, :] = jnp.zeros((8, 128), f32)
        recv_r[1, : 2 * 5 * LEVELS, :] = jnp.zeros((2 * 5 * LEVELS, cols), f32)
        recv_r[1, 2 * 5 * LEVELS :, :] = jnp.ones((2 * ENTRIES - 10 * LEVELS, cols), f32)

    barrier = pltpu.get_barrier_semaphore()

    def greet(dev):
        pl.semaphore_signal(barrier, inc=1, device_id=dev, device_id_type=MESH)

    greet((e_lon, lat))
    greet((w_lon, lat))
    greet((n_lon, n_lat))

    @pl.when(ne_other)
    def _():
        greet((ne_lon, n_lat))

    @pl.when(nw_other)
    def _():
        greet((nw_lon, n_lat))

    @pl.when(inner)
    def _():
        greet((lon, s_lat))
        greet((e_lon, s_lat))
        greet((w_lon, s_lat))

    lane = lax.broadcasted_iota(jnp.int32, (8, 128), 1)
    sub = lax.broadcasted_iota(jnp.int32, (8, 128), 0)
    heights = [jnp.full((8, 128), h_ref[k], f32) for k in range(LEVELS)]
    inv_h2 = [1.0 / (h * h) for h in heights]

    for load in loads:
        load.wait()

    group = lane >> 2

    @pl.loop(0, chunks)
    def _(r):
        span = pl.ds(pl.multiple_of(8 * r, 8), 8)
        held = pl.ds(pl.multiple_of(PAD + 8 * r, 8), 8)
        packed = jnp.zeros((8, 128), f32)
        wet = [wet_i[k, span, :].astype(f32) for k in range(LEVELS)]
        for c in range(ENTRIES):
            ch, k = c // LEVELS, c % LEVELS
            at = c if ch < WET else c + FIELDS
            if ch < WET:
                val = st[at, held, :] * wet[k]
            elif ch == WET:
                val = wet[k]
            elif at == met0:
                val = floor_i[span, :].astype(f32)
            else:
                val = st[at, held, :]
            if at <= met0:
                st[at, held, :] = val
            g = placed(c)
            packed = jnp.where(group == g, pltpu.roll(val, (4 * g + 2) % 128, 1), packed)
        pack[span, :] = packed

    def entries(fn):
        @pl.loop(0, ENTRIES // 4)
        def _(g):
            for i in range(4):
                c = 4 * g + i
                fn(c, c + FIELDS * (g >= FIELDS // 4).astype(jnp.int32))

    def edge_rows(c, at):
        low, high = st[at, pl.ds(PAD, 2), :], st[at, pl.ds(PAD + rows - 2, 2), :]
        send_r[1, pl.ds(2 * c, 2), :] = low
        send_r[0, pl.ds(2 * c, 2), :] = high
        st[at, pl.ds(row0, 2), :] = high
        st[at, pl.ds(row0 + 6, 2), :] = low

    entries(edge_rows)

    @pl.when(top)
    def _():
        @pl.loop(0, 2 * ENTRIES // 8)
        def _(t):
            span = pl.ds(pl.multiple_of(8 * t, 8), 8)
            val = send_r[0, span, :]
            val = jnp.where((sub & 1) == 1, pltpu.roll(val, 1, 0), pltpu.roll(val, 7, 0))
            step = 1
            while step < cols:
                val = jnp.where((lane & step) != 0, pltpu.roll(val, step, 1), pltpu.roll(val, cols - step, 1))
                step *= 2
            flipped = jnp.logical_and(8 * t + sub >= 4 * LEVELS, 8 * t + sub < 8 * LEVELS)
            send_r[0, span, :] = jnp.where(flipped, -val, val)

    last = pack[pl.ds(rows - 8, 8), :]
    turned = jnp.broadcast_to(last[7:8, :], (8, 128))
    for step in (1, 2):
        turned = jnp.where((lane & step) != 0, pltpu.roll(turned, step, 1), pltpu.roll(turned, 128 - step, 1))
    turned = jnp.where(jnp.logical_and(lane >= 8 * LEVELS, lane < 16 * LEVELS), -turned, turned)
    top_v = jnp.full((8, 128), topi) == 1
    folded = jnp.where(top_v, turned, last)
    corner[...] = folded

    @pl.when(ne_self)
    def _():
        ext[0, pl.ds(rows, 8), :] = folded

    @pl.when(nw_self)
    def _():
        ext[1, pl.ds(rows, 8), :] = folded

    pl.semaphore_wait(
        barrier,
        3 + ne_other.astype(jnp.int32) + nw_other.astype(jnp.int32) + 3 * inner.astype(jnp.int32),
    )

    def copy(src, dst, s, r, dev):
        return pltpu.make_async_remote_copy(
            src_ref=src, dst_ref=dst, send_sem=s_sem.at[s], recv_sem=r_sem.at[r], device_id=dev, device_id_type=MESH
        )

    whole, up, down = pl.ds(0, rows), pl.ds(rows, 8), pl.ds(120, 8)
    over = pl.ds(pl.multiple_of(120 - (120 - rows) * topi, 8), 8)
    to_east = copy(pack.at[whole], ext.at[1, whole], 0, 1, (e_lon, lat))
    to_west = copy(pack.at[whole], ext.at[0, whole], 1, 0, (w_lon, lat))
    to_n = copy(send_r.at[0], recv_r.at[1 - topi], 2, 3 - topi, (n_lon, n_lat))
    to_ne = copy(corner, ext.at[1 - topi, over], 4, 7 - 3 * topi, (ne_lon, n_lat))
    to_nw = copy(corner, ext.at[topi, over], 5, 6 - topi, (nw_lon, n_lat))
    to_s = copy(send_r.at[1], recv_r.at[0], 3, 2, (lon, s_lat))
    to_se = copy(pack.at[pl.ds(0, 8)], ext.at[1, up], 6, 5, (e_lon, s_lat))
    to_sw = copy(pack.at[pl.ds(0, 8)], ext.at[0, up], 7, 4, (w_lon, s_lat))
    from_s = copy(send_r.at[0], recv_r.at[1], 2, 3, (lon, s_lat))
    from_se = copy(corner, ext.at[0, down], 5, 6, (e_lon, s_lat))
    from_sw = copy(corner, ext.at[1, down], 4, 7, (w_lon, s_lat))

    to_n.start()
    to_east.start()
    to_west.start()

    @pl.when(ne_other)
    def _():
        to_ne.start()

    @pl.when(nw_other)
    def _():
        to_nw.start()

    @pl.when(inner)
    def _():
        to_s.start()
        to_se.start()
        to_sw.start()

    to_s.wait_recv()

    @pl.when(inner)
    def _():
        from_s.wait_recv()
        from_se.wait_recv()
        from_sw.wait_recv()

    @pl.when(ne_other)
    def _():
        to_sw.wait_recv()

    @pl.when(nw_other)
    def _():
        to_se.wait_recv()

    to_west.wait_recv()
    to_east.wait_recv()

    pair = (lax.broadcasted_iota(jnp.int32, (128, 128), 1) >> 1) & 1

    @pl.loop(0, 2)
    def _(side):
        z[side] = jnp.transpose(jnp.where(pair != side, ext[side], pack[...]))

    def gather(c, at):
        north, south = recv_r[0, pl.ds(2 * c, 2), :], recv_r[1, pl.ds(2 * c, 2), :]
        st[at, pl.ds(PAD + rows, 1), :] = north[0:1, :]
        st[at, pl.ds(PAD - 1, 1), :] = south[1:2, :]
        st[at, pl.ds(row0 + 2, 2), :] = north
        st[at, pl.ds(row0 + 4, 2), :] = south
        st[at, pl.ds(col0, 4), :] = z[0, pl.ds(4 * c, 4), :]
        st[at, pl.ds(col0 + 4, 4), :] = z[1, pl.ds(4 * c, 4), :]

    entries(gather)
    st[met0 + 3, pl.ds(col0, 8), :] = -st[met0 + 3, pl.ds(col0, 8), :]

    is_east = (lane & 3) == 2

    @pl.loop(0, chunks)
    def _(r):
        span = pl.ds(pl.multiple_of(8 * r, 8), 8)
        hold[0, pl.ds(pl.multiple_of(PAD + 8 * r, 8), 8), :] = jnp.where(is_east, ext[0, span, :], ext[1, span, :])

    far_n = jnp.where(is_east, ext[0, up, :], ext[1, up, :])[0:1, :]
    far_s = jnp.where(is_east, ext[0, down, :], ext[1, down, :])[7:8, :]
    hold[0, pl.ds(row0, 8), :] = jnp.where(
        sub == 2, jnp.broadcast_to(far_n, (8, 128)), jnp.broadcast_to(far_s, (8, 128))
    )

    def between():
        @pl.loop(0, 5 * LEVELS // 4)
        def _(g):
            for i in range(4):
                c = 4 * g + i
                at = FIELDS + c
                st[at, pl.ds(PAD + rows, 1), :] = st[at, pl.ds(row0 + 2, 1), :]
                st[at, pl.ds(PAD - 1, 1), :] = st[at, pl.ds(row0 + 5, 1), :]
                z[0, pl.ds(4 * c + 2, 1), :] = st[at, pl.ds(col0 + 2, 1), :]
                z[0, pl.ds(4 * c + 1, 1), :] = st[at, pl.ds(col0 + 5, 1), :]

        hold[1, body, :] = jnp.transpose(z[0])[:rows, :]

    first_step = chunks + 2

    @pl.loop(0, first_step + chunks)
    def _(t):
        pl.when(t == first_step)(between)
        second = (t >= first_step).astype(jnp.int32)
        tile = t - first_step * second
        off = pl.multiple_of(PAD + 8 * (tile + (tile >= chunks).astype(jnp.int32)), 8)
        held = pl.ds(off, 8)
        src = FIELDS * second
        dst = FIELDS - src
        turned_tile = (tile == col_tile).astype(jnp.int32)
        at_first = lane == 0 - turned_tile
        at_last = lane == 127 + turned_tile
        ends_all = hold[second, held, :]

        def side_of(c, val):
            ends = pltpu.roll(ends_all, (126 - 4 * placed(c)) % 128, 1)
            east = pltpu.roll(jnp.where(at_first, ends, val), 127, 1)
            west = pltpu.roll(jnp.where(at_last, ends, val), 1, 1)
            return east, west

        def around(c, at):
            val = st[at, held, :]
            return (val, *side_of(c, val), st[at, pl.ds(off + 1, 8), :], st[at, pl.ds(off - 1, 8), :])

        floor, zs, ms, rot, eddy, *mix = [st[met0 + m, held, :] for m in range(8)]
        rz, rm = 1.0 / zs, 1.0 / ms
        kx, ky, hx, hy = eddy * rz * rz, eddy * rm * rm, 0.5 * rz, 0.5 * rm
        sum_x = sum_y = None
        for k in range(LEVELS):
            wet, we, ww, wn, ws = around(WET * LEVELS + k, wet0 + k)
            dtw = TIME_STEP * wet
            ax, ay = dtw * kx, dtw * ky
            bx, by, br = dtw * hx, dtw * hy, dtw * rot
            ae, aw, an, as_ = ax * we, ax * ww, ay * wn, ay * ws
            centre = 1.0 - (ae + aw) - (an + as_)
            t2 = dtw * inv_h2[k]
            below = above = None
            if k < LEVELS - 1:
                below = t2 * mix[k] * st[wet0 + k + 1, held, :]
                centre = centre - below
            if k > 0:
                above = t2 * mix[k - 1] * st[wet0 + k - 1, held, :]
                centre = centre - above
            drag = centre - jnp.where(floor == float(k), BOTTOM_DRAG * dtw, 0.0)
            u, v = st[src + 2 * LEVELS + k, held, :], st[src + 3 * LEVELS + k, held, :]
            bu, bv = bx * u, by * v
            ce, cw, cn, cs = ae - bu, aw + bu, an - bv, as_ + bv
            layer_x = layer_y = None
            for ch in range(4):
                c = ch * LEVELS + k
                val, east, west, north, south = around(c, src + c)
                new = (centre if ch < 2 else drag) * val + (ce * east + cw * west) + (cn * north + cs * south)
                if below is not None:
                    new = new + below * st[src + c + 1, held, :]
                if above is not None:
                    new = new + above * st[src + c - 1, held, :]
                if ch == 0:
                    layer_x, layer_y = EXPANSION * (west - east), EXPANSION * (south - north)
                if ch == 1:
                    layer_x = (layer_x + CONTRACTION * (east - west)) * heights[k]
                    layer_y = (layer_y + CONTRACTION * (north - south)) * heights[k]
                    sum_x = layer_x if k == 0 else sum_x + layer_x
                    sum_y = layer_y if k == 0 else sum_y + layer_y
                if ch == 2:
                    new = new + br * v - bx * (sum_x - 0.5 * layer_x)
                if ch == 3:
                    new = new - br * u - by * (sum_y - 0.5 * layer_y)
                st[dst + c, held, :] = new

    stores = [pltpu.make_async_copy(st.at[pl.ds(4 * c, 4), body], outs[c], out_sem.at[c]) for c in range(4)]
    for store in stores:
        store.start()

    to_east.wait_send()
    to_west.wait_send()
    to_n.wait_send()

    @pl.when(ne_other)
    def _():
        to_ne.wait_send()

    @pl.when(nw_other)
    def _():
        to_nw.wait_send()

    @pl.when(inner)
    def _():
        to_s.wait_send()
        to_se.wait_send()
        to_sw.wait_send()

    for store in stores:
        store.wait()


def hand_over(*refs):
    moves = []
    for c in range(4):
        for half in range(2):
            part = pl.ds(2 * half, 2)
            moves.append(pltpu.make_async_copy(refs[c].at[part], refs[4 + c].at[part], refs[8].at[2 * c + half]))
    for move in moves:
        move.start()
    for move in moves:
        move.wait()


def solution(mesh):
    nlon, nlat = mesh.shape["lon"], mesh.shape["lat"]

    def shards(*args):
        levels, rows, cols = args[0].shape
        f32 = jnp.float32
        vmem = pltpu.VMEM
        held = rows + 5 * PAD
        hbm = pl.BlockSpec(memory_space=pltpu.HBM)
        out_shape = [jax.ShapeDtypeStruct((levels, rows, cols), f32)] * 4
        results = pl.pallas_call(
            functools.partial(kernel, nlon, nlat, rows, cols),
            out_shape=out_shape,
            in_specs=[hbm] * 11 + [pl.BlockSpec(memory_space=pltpu.SMEM)],
            out_specs=[hbm] * 4,
            scratch_shapes=[
                vmem((2 * FIELDS + ENTRIES - FIELDS, held, cols), f32),
                vmem((2, held, 128), f32),
                vmem((levels, rows, cols), jnp.int32),
                vmem((rows, cols), jnp.int32),
                vmem((128, 128), f32),
                vmem((2, 128, 128), f32),
                vmem((2, 2 * ENTRIES, cols), f32),
                vmem((2, 2 * ENTRIES, cols), f32),
                vmem((8, 128), f32),
                vmem((2, 128, 128), f32),
                pltpu.SemaphoreType.DMA((11,)),
                pltpu.SemaphoreType.DMA((4,)),
                pltpu.SemaphoreType.DMA((8,)),
                pltpu.SemaphoreType.DMA((8,)),
            ],
            compiler_params=pltpu.CompilerParams(
                collective_id=0, has_side_effects=True, vmem_limit_bytes=60 * 1024 * 1024
            ),
        )(*args)
        return tuple(pl.pallas_call(
            hand_over,
            out_shape=out_shape,
            in_specs=[hbm] * 4,
            out_specs=[hbm] * 4,
            scratch_shapes=[pltpu.SemaphoreType.DMA((8,))],
            compiler_params=pltpu.CompilerParams(vmem_limit_bytes=60 * 1024 * 1024),
        )(*results))

    field, plane = P(None, "lat", "lon"), P("lat", "lon")
    return jax.shard_map(
        shards,
        mesh=mesh,
        in_specs=(field,) * 5 + (plane,) * 5 + (field, P()),
        out_specs=(field,) * 4,
        check_vma=False,
    )
```

time: 26.5 us -> 77 us (2.91)
  Pallas kernels: 21.3 us -> 76.2 us
  local copies, waits for them, and re-layouts: 4.33 us -> 0 us
    pallas_call x1, Pallas kernels: 21.3 us -> 51.2 us  [shards(): pl.pallas_call(functools.partial(kernel, nlon, nlat, rows, cols), out_sha...]
    pallas_call x0 -> x1, Pallas kernels: none -> 25 us  [shards(): pl.pallas_call(hand_over, out_shape=out_shape, in_specs=[hbm] * 4, out_sp...]
    unnamed x10 -> x0, local copies, waits for them, and re-layouts: 4.33 us -> none
where the time goes in v3:
time: 77 us; the launch traced here: 76.9 us
  Pallas kernels  76.2 us (99%)
    pallas_call x1, Pallas kernels, shards(): pl.pallas_call(functools.partial(kernel, nlon, nlat, rows, cols), out_sha...  51.2 us
    pallas_call x1, Pallas kernels, shards(): pl.pallas_call(hand_over, out_shape=out_shape, in_specs=[hbm] * 4, out_sp...  25 us

profile of v3, /device:TPU:0, one launch (start us, length us, event | category | flops | bytes accessed | tf_op | source)
XLA Modules:
  0.0 76.9 jit_solution(12008710805933382375)
XLA Ops:
  0.6 51.2 %shard_map.147 = (f32[4,96,128]{2,1,0:T(8,128)}, f32[4,96,128]{2,1,0:T(8,128)}, f32[4,96,128]{2,1,0:T(8,128)}, f32[4,96,128]{2,1,0:T(8,128)}) custom-call(f32[4,96,128]{2,1,0:T(8,128)} %refs_0_.1, f32[4,96,128]{2,1,0:T(8,128)} %refs_1_.1, f32[4,96,128]{2,1,0:T(8,128)} %refs_2_.1, f32[4,96,128]{2,1,0:T(8,128)} %refs_3_.1, s32[4,96,128]{2,1,0:T(8,128)} %refs_4_.1, ...), custom_call_target="tpu_custom_call" | custom-call | tf_op jit(solution)/shard_map/pallas_call | solution.py:398
  51.9 25.0 %shard_map.148 = (f32[4,96,128]{2,1,0:T(8,128)}, f32[4,96,128]{2,1,0:T(8,128)}, f32[4,96,128]{2,1,0:T(8,128)}, f32[4,96,128]{2,1,0:T(8,128)}) custom-call(f32[4,96,128]{2,1,0:T(8,128)} %get-tuple-element.8.refs_0_, f32[4,96,128]{2,1,0:T(8,128)} %get-tuple-element.9.refs_1_, f32[4,96,128]{2,1,0:T(8,128)} %get-tuple-element.10.refs_2_, ...), custom_call_target="tpu_custom_call" | custom-call | tf_op jit(solution)/shard_map/pallas_call | solution.py:423

commit v4 on v3

--- a/solution.py
+++ b/solution.py
@@ -106,6 +106,7 @@
         span = pl.ds(pl.multiple_of(8 * r, 8), 8)
         held = pl.ds(pl.multiple_of(PAD + 8 * r, 8), 8)
         packed = jnp.zeros((8, 128), f32)
+        kept = []
         wet = [wet_i[k, span, :].astype(f32) for k in range(LEVELS)]
         for c in range(ENTRIES):
             ch, k = c // LEVELS, c % LEVELS
@@ -119,26 +120,31 @@
             else:
                 val = st[at, held, :]
             if at <= met0:
-                st[at, held, :] = val
+                kept.append((at, val))
             g = placed(c)
             packed = jnp.where(group == g, pltpu.roll(val, (4 * g + 2) % 128, 1), packed)
         pack[span, :] = packed
-
-    def entries(fn):
+        for at, val in kept:
+            st[at, held, :] = val
+
+    def entries(load, save):
         @pl.loop(0, ENTRIES // 4)
         def _(g):
+            at = 4 * g + FIELDS * (g >= FIELDS // 4).astype(jnp.int32)
+            held = [load(4 * g + i, at + i) for i in range(4)]
             for i in range(4):
-                c = 4 * g + i
-                fn(c, c + FIELDS * (g >= FIELDS // 4).astype(jnp.int32))
-
-    def edge_rows(c, at):
-        low, high = st[at, pl.ds(PAD, 2), :], st[at, pl.ds(PAD + rows - 2, 2), :]
+                save(4 * g + i, at + i, *held[i])
+
+    def take_edges(c, at):
+        return st[at, pl.ds(PAD, 2), :], st[at, pl.ds(PAD + rows - 2, 2), :]
+
+    def put_edges(c, at, low, high):
         send_r[1, pl.ds(2 * c, 2), :] = low
         send_r[0, pl.ds(2 * c, 2), :] = high
         st[at, pl.ds(row0, 2), :] = high
         st[at, pl.ds(row0 + 6, 2), :] = low
 
-    entries(edge_rows)
+    entries(take_edges, put_edges)
 
     @pl.when(top)
     def _():
@@ -238,16 +244,19 @@
     def _(side):
         z[side] = jnp.transpose(jnp.where(pair != side, ext[side], pack[...]))
 
-    def gather(c, at):
-        north, south = recv_r[0, pl.ds(2 * c, 2), :], recv_r[1, pl.ds(2 * c, 2), :]
+    def take_halo(c, at):
+        two, four = pl.ds(2 * c, 2), pl.ds(4 * c, 4)
+        return recv_r[0, two, :], recv_r[1, two, :], z[0, four, :], z[1, four, :]
+
+    def put_halo(c, at, north, south, east, west):
         st[at, pl.ds(PAD + rows, 1), :] = north[0:1, :]
         st[at, pl.ds(PAD - 1, 1), :] = south[1:2, :]
         st[at, pl.ds(row0 + 2, 2), :] = north
         st[at, pl.ds(row0 + 4, 2), :] = south
-        st[at, pl.ds(col0, 4), :] = z[0, pl.ds(4 * c, 4), :]
-        st[at, pl.ds(col0 + 4, 4), :] = z[1, pl.ds(4 * c, 4), :]
-
-    entries(gather)
+        st[at, pl.ds(col0, 4), :] = east
+        st[at, pl.ds(col0 + 4, 4), :] = west
+
+    entries(take_halo, put_halo)
     st[met0 + 3, pl.ds(col0, 8), :] = -st[met0 + 3, pl.ds(col0, 8), :]
 
     is_east = (lane & 3) == 2
@@ -266,13 +275,13 @@
     def between():
         @pl.loop(0, 5 * LEVELS // 4)
         def _(g):
-            for i in range(4):
+            held = [(st[FIELDS + 4 * g + i, pl.ds(row0, 8), :], st[FIELDS + 4 * g + i, pl.ds(col0, 8), :]) for i in range(4)]
+            for i, (about_row, about_col) in enumerate(held):
                 c = 4 * g + i
-                at = FIELDS + c
-                st[at, pl.ds(PAD + rows, 1), :] = st[at, pl.ds(row0 + 2, 1), :]
-                st[at, pl.ds(PAD - 1, 1), :] = st[at, pl.ds(row0 + 5, 1), :]
-                z[0, pl.ds(4 * c + 2, 1), :] = st[at, pl.ds(col0 + 2, 1), :]
-                z[0, pl.ds(4 * c + 1, 1), :] = st[at, pl.ds(col0 + 5, 1), :]
+                st[FIELDS + c, pl.ds(PAD + rows, 1), :] = about_row[2:3, :]
+                st[FIELDS + c, pl.ds(PAD - 1, 1), :] = about_row[5:6, :]
+                z[0, pl.ds(4 * c + 2, 1), :] = about_col[2:3, :]
+                z[0, pl.ds(4 * c + 1, 1), :] = about_col[5:6, :]
 
         hold[1, body, :] = jnp.transpose(z[0])[:rows, :]
 
@@ -305,6 +314,7 @@
         floor, zs, ms, rot, eddy, *mix = [st[met0 + m, held, :] for m in range(8)]
         rz, rm = 1.0 / zs, 1.0 / ms
         kx, ky, hx, hy = eddy * rz * rz, eddy * rm * rm, 0.5 * rz, 0.5 * rm
+        results = []
         sum_x = sum_y = None
         for k in range(LEVELS):
             wet, we, ww, wn, ws = around(WET * LEVELS + k, wet0 + k)
@@ -345,7 +355,9 @@
                     new = new + br * v - bx * (sum_x - 0.5 * layer_x)
                 if ch == 3:
                     new = new - br * u - by * (sum_y - 0.5 * layer_y)
-                st[dst + c, held, :] = new
+                results.append((c, new))
+        for c, new in results:
+            st[dst + c, held, :] = new
 
     stores = [pltpu.make_async_copy(st.at[pl.ds(4 * c, 4), body], outs[c], out_sem.at[c]) for c in range(4)]
     for store in stores:
@@ -374,15 +386,16 @@
 
 
 def hand_over(*refs):
-    moves = []
-    for c in range(4):
-        for half in range(2):
-            part = pl.ds(2 * half, 2)
-            moves.append(pltpu.make_async_copy(refs[c].at[part], refs[4 + c].at[part], refs[8].at[2 * c + half]))
+    held, sem_in, sem_out = refs[8:]
+    moves = [pltpu.make_async_copy(refs[c], held.at[c], sem_in.at[c]) for c in range(4)]
+    stores = [pltpu.make_async_copy(held.at[c], refs[4 + c], sem_out.at[c]) for c in range(4)]
     for move in moves:
         move.start()
-    for move in moves:
+    for move, store in zip(moves, stores):
         move.wait()
+        store.start()
+    for store in stores:
+        store.wait()
 
 
 def solution(mesh):
@@ -425,7 +438,7 @@
             out_shape=out_shape,
             in_specs=[hbm] * 4,
             out_specs=[hbm] * 4,
-            scratch_shapes=[pltpu.SemaphoreType.DMA((8,))],
+            scratch_shapes=[vmem((4, levels, rows, cols), f32), pltpu.SemaphoreType.DMA((4,)), pltpu.SemaphoreType.DMA((4,))],
             compiler_params=pltpu.CompilerParams(vmem_limit_bytes=60 * 1024 * 1024),
         )(*results))
 

time: 77 us -> 25 us (0.32)
  Pallas kernels: 76.2 us -> 24.2 us
    pallas_call x1, Pallas kernels: 51.2 us -> 22.2 us  [shards(): pl.pallas_call(functools.partial(kernel, nlon, nlat, rows, cols), out_sha...]
    pallas_call x1, Pallas kernels: 25 us -> 1.96 us  [shards(): pl.pallas_call(hand_over, out_shape=out_shape, in_specs=[hbm] * 4, out_sp...]
where the time goes in v4:
time: 25 us; the launch traced here: 24.8 us
  Pallas kernels  24.2 us (97%)
  between operations  0.64 us (3%)
    pallas_call x1, Pallas kernels, shards(): pl.pallas_call(functools.partial(kernel, nlon, nlat, rows, cols), out_sha...  22.2 us
    pallas_call x1, Pallas kernels, shards(): pl.pallas_call(hand_over, out_shape=out_shape, in_specs=[hbm] * 4, out_sp...  1.96 us

profile of v4, /device:TPU:0, one launch (start us, length us, event | category | flops | bytes accessed | tf_op | source)
XLA Modules:
  0.0 24.8 jit_solution(7364897990476394510)
XLA Ops:
  0.6 22.2 %shard_map.147 = (f32[4,96,128]{2,1,0:T(8,128)}, f32[4,96,128]{2,1,0:T(8,128)}, f32[4,96,128]{2,1,0:T(8,128)}, f32[4,96,128]{2,1,0:T(8,128)}) custom-call(f32[4,96,128]{2,1,0:T(8,128)} %refs_0_.1, f32[4,96,128]{2,1,0:T(8,128)} %refs_1_.1, f32[4,96,128]{2,1,0:T(8,128)} %refs_2_.1, f32[4,96,128]{2,1,0:T(8,128)} %refs_3_.1, s32[4,96,128]{2,1,0:T(8,128)} %refs_4_.1, ...), custom_call_target="tpu_custom_call" | custom-call | tf_op jit(solution)/shard_map/pallas_call | solution.py:411
  22.9 2.0 %shard_map.148 = (f32[4,96,128]{2,1,0:T(8,128)}, f32[4,96,128]{2,1,0:T(8,128)}, f32[4,96,128]{2,1,0:T(8,128)}, f32[4,96,128]{2,1,0:T(8,128)}) custom-call(f32[4,96,128]{2,1,0:T(8,128)} %get-tuple-element.8.refs_0_, f32[4,96,128]{2,1,0:T(8,128)} %get-tuple-element.9.refs_1_, f32[4,96,128]{2,1,0:T(8,128)} %get-tuple-element.10.refs_2_, ...), custom_call_target="tpu_custom_call" | custom-call | tf_op jit(solution)/shard_map/pallas_call | solution.py:436

commit v5 on v4

--- a/solution.py
+++ b/solution.py
@@ -148,17 +148,15 @@
 
     @pl.when(top)
     def _():
-        @pl.loop(0, 2 * ENTRIES // 8)
-        def _(t):
-            span = pl.ds(pl.multiple_of(8 * t, 8), 8)
-            val = send_r[0, span, :]
-            val = jnp.where((sub & 1) == 1, pltpu.roll(val, 1, 0), pltpu.roll(val, 7, 0))
-            step = 1
-            while step < cols:
-                val = jnp.where((lane & step) != 0, pltpu.roll(val, step, 1), pltpu.roll(val, cols - step, 1))
-                step *= 2
-            flipped = jnp.logical_and(8 * t + sub >= 4 * LEVELS, 8 * t + sub < 8 * LEVELS)
-            send_r[0, span, :] = jnp.where(flipped, -val, val)
+        tiles = [send_r[0, pl.ds(8 * t, 8), :] for t in range(2 * ENTRIES // 8)]
+        tiles = [jnp.where((sub & 1) == 1, pltpu.roll(v, 1, 0), pltpu.roll(v, 7, 0)) for v in tiles]
+        step = 1
+        while step < cols:
+            far_half = (lane & step) != 0
+            tiles = [jnp.where(far_half, pltpu.roll(v, step, 1), pltpu.roll(v, cols - step, 1)) for v in tiles]
+            step *= 2
+        for t, v in enumerate(tiles):
+            send_r[0, pl.ds(8 * t, 8), :] = -v if 4 * LEVELS <= 8 * t < 8 * LEVELS else v
 
     last = pack[pl.ds(rows - 8, 8), :]
     turned = jnp.broadcast_to(last[7:8, :], (8, 128))
@@ -219,58 +217,59 @@
         to_se.start()
         to_sw.start()
 
-    to_s.wait_recv()
-
-    @pl.when(inner)
-    def _():
-        from_s.wait_recv()
-        from_se.wait_recv()
-        from_sw.wait_recv()
-
-    @pl.when(ne_other)
-    def _():
-        to_sw.wait_recv()
-
-    @pl.when(nw_other)
-    def _():
-        to_se.wait_recv()
-
-    to_west.wait_recv()
-    to_east.wait_recv()
-
-    pair = (lax.broadcasted_iota(jnp.int32, (128, 128), 1) >> 1) & 1
-
-    @pl.loop(0, 2)
-    def _(side):
-        z[side] = jnp.transpose(jnp.where(pair != side, ext[side], pack[...]))
-
-    def take_halo(c, at):
-        two, four = pl.ds(2 * c, 2), pl.ds(4 * c, 4)
-        return recv_r[0, two, :], recv_r[1, two, :], z[0, four, :], z[1, four, :]
-
-    def put_halo(c, at, north, south, east, west):
-        st[at, pl.ds(PAD + rows, 1), :] = north[0:1, :]
-        st[at, pl.ds(PAD - 1, 1), :] = south[1:2, :]
-        st[at, pl.ds(row0 + 2, 2), :] = north
-        st[at, pl.ds(row0 + 4, 2), :] = south
-        st[at, pl.ds(col0, 4), :] = east
-        st[at, pl.ds(col0 + 4, 4), :] = west
-
-    entries(take_halo, put_halo)
-    st[met0 + 3, pl.ds(col0, 8), :] = -st[met0 + 3, pl.ds(col0, 8), :]
-
     is_east = (lane & 3) == 2
 
-    @pl.loop(0, chunks)
-    def _(r):
-        span = pl.ds(pl.multiple_of(8 * r, 8), 8)
-        hold[0, pl.ds(pl.multiple_of(PAD + 8 * r, 8), 8), :] = jnp.where(is_east, ext[0, span, :], ext[1, span, :])
-
-    far_n = jnp.where(is_east, ext[0, up, :], ext[1, up, :])[0:1, :]
-    far_s = jnp.where(is_east, ext[0, down, :], ext[1, down, :])[7:8, :]
-    hold[0, pl.ds(row0, 8), :] = jnp.where(
-        sub == 2, jnp.broadcast_to(far_n, (8, 128)), jnp.broadcast_to(far_s, (8, 128))
-    )
+    def arrive():
+        to_s.wait_recv()
+
+        @pl.when(inner)
+        def _():
+            from_s.wait_recv()
+            from_se.wait_recv()
+            from_sw.wait_recv()
+
+        @pl.when(ne_other)
+        def _():
+            to_sw.wait_recv()
+
+        @pl.when(nw_other)
+        def _():
+            to_se.wait_recv()
+
+        to_west.wait_recv()
+        to_east.wait_recv()
+
+        pair = (lax.broadcasted_iota(jnp.int32, (128, 128), 1) >> 1) & 1
+
+        @pl.loop(0, 2)
+        def _(side):
+            z[side] = jnp.transpose(jnp.where(pair != side, ext[side], pack[...]))
+
+        def take_halo(c, at):
+            two, four = pl.ds(2 * c, 2), pl.ds(4 * c, 4)
+            return recv_r[0, two, :], recv_r[1, two, :], z[0, four, :], z[1, four, :]
+
+        def put_halo(c, at, north, south, east, west):
+            st[at, pl.ds(PAD + rows, 1), :] = north[0:1, :]
+            st[at, pl.ds(PAD - 1, 1), :] = south[1:2, :]
+            st[at, pl.ds(row0 + 2, 2), :] = north
+            st[at, pl.ds(row0 + 4, 2), :] = south
+            st[at, pl.ds(col0, 4), :] = east
+            st[at, pl.ds(col0 + 4, 4), :] = west
+
+        entries(take_halo, put_halo)
+        st[met0 + 3, pl.ds(col0, 8), :] = -st[met0 + 3, pl.ds(col0, 8), :]
+
+        @pl.loop(0, chunks)
+        def _(r):
+            span = pl.ds(pl.multiple_of(8 * r, 8), 8)
+            hold[0, pl.ds(pl.multiple_of(PAD + 8 * r, 8), 8), :] = jnp.where(is_east, ext[0, span, :], ext[1, span, :])
+
+        far_n = jnp.where(is_east, ext[0, up, :], ext[1, up, :])[0:1, :]
+        far_s = jnp.where(is_east, ext[0, down, :], ext[1, down, :])[7:8, :]
+        hold[0, pl.ds(row0, 8), :] = jnp.where(
+            sub == 2, jnp.broadcast_to(far_n, (8, 128)), jnp.broadcast_to(far_s, (8, 128))
+        )
 
     def between():
         @pl.loop(0, 5 * LEVELS // 4)
@@ -282,21 +281,39 @@
                 st[FIELDS + c, pl.ds(PAD - 1, 1), :] = about_row[5:6, :]
                 z[0, pl.ds(4 * c + 2, 1), :] = about_col[2:3, :]
                 z[0, pl.ds(4 * c + 1, 1), :] = about_col[5:6, :]
+                z[1, pl.ds(4 * c + 2, 1), :] = about_col[6:7, :]
+                z[1, pl.ds(4 * c + 1, 1), :] = about_col[1:2, :]
 
         hold[1, body, :] = jnp.transpose(z[0])[:rows, :]
-
-    first_step = chunks + 2
-
-    @pl.loop(0, first_step + chunks)
-    def _(t):
-        pl.when(t == first_step)(between)
-        second = (t >= first_step).astype(jnp.int32)
-        tile = t - first_step * second
-        off = pl.multiple_of(PAD + 8 * (tile + (tile >= chunks).astype(jnp.int32)), 8)
+        hold[0, body, :] = jnp.transpose(z[1])[:rows, :]
+
+        @pl.loop(1, chunks - 1)
+        def _(r):
+            held = pl.ds(pl.multiple_of(PAD + 8 * r, 8), 8)
+            own = hold[0, held, :]
+            outer = jnp.logical_or(lane == 0, lane == 127)
+            vals = [st[FIELDS + c, held, :] for c in range(FIELDS)]
+            for c in range(FIELDS):
+                ends = pltpu.roll(own, (126 - 4 * placed(c)) % 128, 1)
+                st[FIELDS + c, held, :] = jnp.where(outer, ends, vals[c])
+
+    ahead = (chunks - 2) // 2
+    flag = lambda cond: cond.astype(jnp.int32)
+
+    def tile_values(p, i):
+        second = flag(p >= ahead + 2)
+        early = flag(p < ahead)
+        outer = flag(p == ahead)
+        slabs = flag(p == ahead + 1)
+        tile = (
+            early * (1 + 2 * p + i) + outer * (i * (chunks - 1)) + slabs * (chunks + i)
+            + second * (2 * (p - ahead - 2) + i)
+        )
+        off = pl.multiple_of(PAD + 8 * (tile + slabs), 8)
         held = pl.ds(off, 8)
         src = FIELDS * second
         dst = FIELDS - src
-        turned_tile = (tile == col_tile).astype(jnp.int32)
+        turned_tile = early + slabs * i
         at_first = lane == 0 - turned_tile
         at_last = lane == 127 + turned_tile
         ends_all = hold[second, held, :]
@@ -356,8 +373,16 @@
                 if ch == 3:
                     new = new - br * u - by * (sum_y - 0.5 * layer_y)
                 results.append((c, new))
-        for c, new in results:
-            st[dst + c, held, :] = new
+        return dst, held, results
+
+    @pl.loop(0, ahead + 2 + chunks // 2)
+    def _(p):
+        pl.when(p == ahead)(arrive)
+        pl.when(p == ahead + 2)(between)
+        done = [tile_values(p, i) for i in range(2)]
+        for dst, held, results in done:
+            for c, new in results:
+                st[dst + c, held, :] = new
 
     stores = [pltpu.make_async_copy(st.at[pl.ds(4 * c, 4), body], outs[c], out_sem.at[c]) for c in range(4)]
     for store in stores:

time: 25 us -> 20.6 us (0.82)
  Pallas kernels: 24.2 us -> 19.8 us
    pallas_call x1, Pallas kernels: 22.2 us -> 17.8 us  [shards(): pl.pallas_call(functools.partial(kernel, nlon, nlat, rows, cols), out_sha...]
where the time goes in v5:
time: 20.6 us; the launch traced here: 20.4 us
  Pallas kernels  19.8 us (96%)
  between operations  0.64 us (3%)
    pallas_call x1, Pallas kernels, shards(): pl.pallas_call(functools.partial(kernel, nlon, nlat, rows, cols), out_sha...  17.8 us
    pallas_call x1, Pallas kernels, shards(): pl.pallas_call(hand_over, out_shape=out_shape, in_specs=[hbm] * 4, out_sp...  1.96 us

profile of v5, /device:TPU:0, one launch (start us, length us, event | category | flops | bytes accessed | tf_op | source)
XLA Modules:
  0.0 20.4 jit_solution(11773112907306586205)
XLA Ops:
  0.6 17.8 %shard_map.147 = (f32[4,96,128]{2,1,0:T(8,128)}, f32[4,96,128]{2,1,0:T(8,128)}, f32[4,96,128]{2,1,0:T(8,128)}, f32[4,96,128]{2,1,0:T(8,128)}) custom-call(f32[4,96,128]{2,1,0:T(8,128)} %refs_0_.1, f32[4,96,128]{2,1,0:T(8,128)} %refs_1_.1, f32[4,96,128]{2,1,0:T(8,128)} %refs_2_.1, f32[4,96,128]{2,1,0:T(8,128)} %refs_3_.1, s32[4,96,128]{2,1,0:T(8,128)} %refs_4_.1, ...), custom_call_target="tpu_custom_call" | custom-call | tf_op jit(solution)/shard_map/pallas_call | solution.py:436
  18.5 2.0 %shard_map.148 = (f32[4,96,128]{2,1,0:T(8,128)}, f32[4,96,128]{2,1,0:T(8,128)}, f32[4,96,128]{2,1,0:T(8,128)}, f32[4,96,128]{2,1,0:T(8,128)}) custom-call(f32[4,96,128]{2,1,0:T(8,128)} %get-tuple-element.8.refs_0_, f32[4,96,128]{2,1,0:T(8,128)} %get-tuple-element.9.refs_1_, f32[4,96,128]{2,1,0:T(8,128)} %get-tuple-element.10.refs_2_, ...), custom_call_target="tpu_custom_call" | custom-call | tf_op jit(solution)/shard_map/pallas_call | solution.py:461

commit v6 on v5

--- a/solution.py
+++ b/solution.py
@@ -30,7 +30,7 @@
 def kernel(nlon, nlat, rows, cols, *refs):
     ins, h_ref = refs[:11], refs[11]
     outs = refs[12:16]
-    (st, hold, wet_i, floor_i, pack, ext, send_r, recv_r, corner, z, in_sem, out_sem, s_sem, r_sem) = refs[16:]
+    (st, hold, wet_i, floor_i, pack, ext, send_r, recv_r, corner, z, in_sem, s_sem, r_sem) = refs[16:]
     lon, lat = lax.axis_index("lon"), lax.axis_index("lat")
     top, bottom = lat == nlat - 1, lat == 0
     topi = top.astype(jnp.int32)
@@ -101,8 +101,7 @@
 
     group = lane >> 2
 
-    @pl.loop(0, chunks)
-    def _(r):
+    def masked(r):
         span = pl.ds(pl.multiple_of(8 * r, 8), 8)
         held = pl.ds(pl.multiple_of(PAD + 8 * r, 8), 8)
         packed = jnp.zeros((8, 128), f32)
@@ -123,9 +122,14 @@
                 kept.append((at, val))
             g = placed(c)
             packed = jnp.where(group == g, pltpu.roll(val, (4 * g + 2) % 128, 1), packed)
-        pack[span, :] = packed
-        for at, val in kept:
-            st[at, held, :] = val
+        return span, held, packed, kept
+
+    @pl.loop(0, chunks // 2)
+    def _(r):
+        for span, held, packed, kept in [masked(2 * r + i) for i in range(2)]:
+            pack[span, :] = packed
+            for at, val in kept:
+                st[at, held, :] = val
 
     def entries(load, save):
         @pl.loop(0, ENTRIES // 4)
@@ -287,15 +291,18 @@
         hold[1, body, :] = jnp.transpose(z[0])[:rows, :]
         hold[0, body, :] = jnp.transpose(z[1])[:rows, :]
 
-        @pl.loop(1, chunks - 1)
+        @pl.loop(0, (chunks - 2) // 2)
         def _(r):
-            held = pl.ds(pl.multiple_of(PAD + 8 * r, 8), 8)
-            own = hold[0, held, :]
             outer = jnp.logical_or(lane == 0, lane == 127)
-            vals = [st[FIELDS + c, held, :] for c in range(FIELDS)]
-            for c in range(FIELDS):
-                ends = pltpu.roll(own, (126 - 4 * placed(c)) % 128, 1)
-                st[FIELDS + c, held, :] = jnp.where(outer, ends, vals[c])
+            patched = []
+            for i in range(2):
+                held = pl.ds(pl.multiple_of(PAD + 8 * (1 + 2 * r + i), 8), 8)
+                own = hold[0, held, :]
+                for c in range(FIELDS):
+                    ends = pltpu.roll(own, (126 - 4 * placed(c)) % 128, 1)
+                    patched.append((c, held, jnp.where(outer, ends, st[FIELDS + c, held, :])))
+            for c, held, val in patched:
+                st[FIELDS + c, held, :] = val
 
     ahead = (chunks - 2) // 2
     flag = lambda cond: cond.astype(jnp.int32)
@@ -384,9 +391,12 @@
             for c, new in results:
                 st[dst + c, held, :] = new
 
-    stores = [pltpu.make_async_copy(st.at[pl.ds(4 * c, 4), body], outs[c], out_sem.at[c]) for c in range(4)]
-    for store in stores:
-        store.start()
+    @pl.loop(0, chunks)
+    def _(r):
+        held = pl.ds(pl.multiple_of(PAD + 8 * r, 8), 8)
+        vals = [st[c, held, :] for c in range(FIELDS)]
+        for c in range(FIELDS):
+            outs[c // LEVELS][c % LEVELS, pl.ds(pl.multiple_of(8 * r, 8), 8), :] = vals[c]
 
     to_east.wait_send()
     to_west.wait_send()
@@ -406,21 +416,13 @@
         to_se.wait_send()
         to_sw.wait_send()
 
-    for store in stores:
-        store.wait()
-
 
 def hand_over(*refs):
-    held, sem_in, sem_out = refs[8:]
-    moves = [pltpu.make_async_copy(refs[c], held.at[c], sem_in.at[c]) for c in range(4)]
-    stores = [pltpu.make_async_copy(held.at[c], refs[4 + c], sem_out.at[c]) for c in range(4)]
+    moves = [pltpu.make_async_copy(refs[c], refs[4 + c], refs[8].at[c]) for c in range(4)]
     for move in moves:
         move.start()
-    for move, store in zip(moves, stores):
+    for move in moves:
         move.wait()
-        store.start()
-    for store in stores:
-        store.wait()
 
 
 def solution(mesh):
@@ -435,9 +437,9 @@
         out_shape = [jax.ShapeDtypeStruct((levels, rows, cols), f32)] * 4
         results = pl.pallas_call(
             functools.partial(kernel, nlon, nlat, rows, cols),
-            out_shape=out_shape,
+            out_shape=[pltpu.VMEM((levels, rows, cols), f32)] * 4,
             in_specs=[hbm] * 11 + [pl.BlockSpec(memory_space=pltpu.SMEM)],
-            out_specs=[hbm] * 4,
+            out_specs=[pl.BlockSpec(memory_space=pltpu.VMEM)] * 4,
             scratch_shapes=[
                 vmem((2 * FIELDS + ENTRIES - FIELDS, held, cols), f32),
                 vmem((2, held, 128), f32),
@@ -450,7 +452,6 @@
                 vmem((8, 128), f32),
                 vmem((2, 128, 128), f32),
                 pltpu.SemaphoreType.DMA((11,)),
-                pltpu.SemaphoreType.DMA((4,)),
                 pltpu.SemaphoreType.DMA((8,)),
                 pltpu.SemaphoreType.DMA((8,)),
             ],
@@ -461,10 +462,10 @@
         return tuple(pl.pallas_call(
             hand_over,
             out_shape=out_shape,
-            in_specs=[hbm] * 4,
+            in_specs=[pl.BlockSpec(memory_space=pltpu.VMEM)] * 4,
             out_specs=[hbm] * 4,
-            scratch_shapes=[vmem((4, levels, rows, cols), f32), pltpu.SemaphoreType.DMA((4,)), pltpu.SemaphoreType.DMA((4,))],
-            compiler_params=pltpu.CompilerParams(vmem_limit_bytes=60 * 1024 * 1024),
+            scratch_shapes=[pltpu.SemaphoreType.DMA((4,))],
+            compiler_params=pltpu.CompilerParams(vmem_limit_bytes=16 * 1024 * 1024),
         )(*results))
 
     field, plane = P(None, "lat", "lon"), P("lat", "lon")

time: 20.6 us -> 18 us (0.87)
  Pallas kernels: 19.8 us -> 17.2 us
    pallas_call x1, Pallas kernels: 17.8 us -> 16.3 us  [shards(): pl.pallas_call(functools.partial(kernel, nlon, nlat, rows, cols), out_sha...]
    pallas_call x1, Pallas kernels: 1.96 us -> 0.91 us  [shards(): pl.pallas_call(hand_over, out_shape=out_shape, in_specs=[pl.BlockSpec(mem...]
where the time goes in v6:
time: 18 us; the launch traced here: 17.8 us
  Pallas kernels  17.2 us (96%)
  between operations  0.64 us (4%)
    pallas_call x1, Pallas kernels, shards(): pl.pallas_call(functools.partial(kernel, nlon, nlat, rows, cols), out_sha...  16.3 us
    pallas_call x1, Pallas kernels, shards(): pl.pallas_call(hand_over, out_shape=out_shape, in_specs=[pl.BlockSpec(mem...  0.91 us

profile of v6, /device:TPU:0, one launch (start us, length us, event | category | flops | bytes accessed | tf_op | source)
XLA Modules:
  0.0 17.8 jit_solution(9003183744492138534)
XLA Ops:
  0.6 16.3 %shard_map.147 = (f32[4,96,128]{2,1,0:T(8,128)S(1)}, f32[4,96,128]{2,1,0:T(8,128)S(1)}, f32[4,96,128]{2,1,0:T(8,128)S(1)}, f32[4,96,128]{2,1,0:T(8,128)S(1)}) custom-call(f32[4,96,128]{2,1,0:T(8,128)} %refs_0_.1, f32[4,96,128]{2,1,0:T(8,128)} %refs_1_.1, f32[4,96,128]{2,1,0:T(8,128)} %refs_2_.1, f32[4,96,128]{2,1,0:T(8,128)} %refs_3_.1, ...), custom_call_target="tpu_custom_call" | custom-call | tf_op jit(solution)/shard_map/pallas_call | solution.py:438
  16.9 0.9 %shard_map.148 = (f32[4,96,128]{2,1,0:T(8,128)}, f32[4,96,128]{2,1,0:T(8,128)}, f32[4,96,128]{2,1,0:T(8,128)}, f32[4,96,128]{2,1,0:T(8,128)}) custom-call(f32[4,96,128]{2,1,0:T(8,128)S(1)} %get-tuple-element.8.refs_0_, f32[4,96,128]{2,1,0:T(8,128)S(1)} %get-tuple-element.9.refs_1_, f32[4,96,128]{2,1,0:T(8,128)S(1)} %get-tuple-element.10.refs_2_, ...), custom_call_target="tpu_custom_call" | custom-call | tf_op jit(solution)/shard_map/pallas_call | solution.py:462

commit v7 on v6

--- a/solution.py
+++ b/solution.py
@@ -139,29 +139,6 @@
             for i in range(4):
                 save(4 * g + i, at + i, *held[i])
 
-    def take_edges(c, at):
-        return st[at, pl.ds(PAD, 2), :], st[at, pl.ds(PAD + rows - 2, 2), :]
-
-    def put_edges(c, at, low, high):
-        send_r[1, pl.ds(2 * c, 2), :] = low
-        send_r[0, pl.ds(2 * c, 2), :] = high
-        st[at, pl.ds(row0, 2), :] = high
-        st[at, pl.ds(row0 + 6, 2), :] = low
-
-    entries(take_edges, put_edges)
-
-    @pl.when(top)
-    def _():
-        tiles = [send_r[0, pl.ds(8 * t, 8), :] for t in range(2 * ENTRIES // 8)]
-        tiles = [jnp.where((sub & 1) == 1, pltpu.roll(v, 1, 0), pltpu.roll(v, 7, 0)) for v in tiles]
-        step = 1
-        while step < cols:
-            far_half = (lane & step) != 0
-            tiles = [jnp.where(far_half, pltpu.roll(v, step, 1), pltpu.roll(v, cols - step, 1)) for v in tiles]
-            step *= 2
-        for t, v in enumerate(tiles):
-            send_r[0, pl.ds(8 * t, 8), :] = -v if 4 * LEVELS <= 8 * t < 8 * LEVELS else v
-
     last = pack[pl.ds(rows - 8, 8), :]
     turned = jnp.broadcast_to(last[7:8, :], (8, 128))
     for step in (1, 2):
@@ -203,7 +180,6 @@
     from_se = copy(corner, ext.at[0, down], 5, 6, (e_lon, s_lat))
     from_sw = copy(corner, ext.at[1, down], 4, 7, (w_lon, s_lat))
 
-    to_n.start()
     to_east.start()
     to_west.start()
 
@@ -217,9 +193,37 @@
 
     @pl.when(inner)
     def _():
-        to_s.start()
         to_se.start()
         to_sw.start()
+
+    def take_edges(c, at):
+        return st[at, pl.ds(PAD, 2), :], st[at, pl.ds(PAD + rows - 2, 2), :]
+
+    def put_edges(c, at, low, high):
+        send_r[1, pl.ds(2 * c, 2), :] = low
+        send_r[0, pl.ds(2 * c, 2), :] = high
+        st[at, pl.ds(row0, 2), :] = high
+        st[at, pl.ds(row0 + 6, 2), :] = low
+
+    entries(take_edges, put_edges)
+
+    @pl.when(top)
+    def _():
+        tiles = [send_r[0, pl.ds(8 * t, 8), :] for t in range(2 * ENTRIES // 8)]
+        tiles = [jnp.where((sub & 1) == 1, pltpu.roll(v, 1, 0), pltpu.roll(v, 7, 0)) for v in tiles]
+        step = 1
+        while step < cols:
+            far_half = (lane & step) != 0
+            tiles = [jnp.where(far_half, pltpu.roll(v, step, 1), pltpu.roll(v, cols - step, 1)) for v in tiles]
+            step *= 2
+        for t, v in enumerate(tiles):
+            send_r[0, pl.ds(8 * t, 8), :] = -v if 4 * LEVELS <= 8 * t < 8 * LEVELS else v
+
+    to_n.start()
+
+    @pl.when(inner)
+    def _():
+        to_s.start()
 
     is_east = (lane & 3) == 2
 
@@ -245,9 +249,10 @@
 
         pair = (lax.broadcasted_iota(jnp.int32, (128, 128), 1) >> 1) & 1
 
-        @pl.loop(0, 2)
-        def _(side):
-            z[side] = jnp.transpose(jnp.where(pair != side, ext[side], pack[...]))
+        own = pack[...]
+        about = [jnp.transpose(jnp.where(pair != side, ext[side], own)) for side in range(2)]
+        for side in range(2):
+            z[side] = about[side]
 
         def take_halo(c, at):
             two, four = pl.ds(2 * c, 2), pl.ds(4 * c, 4)
@@ -391,12 +396,12 @@
             for c, new in results:
                 st[dst + c, held, :] = new
 
-    @pl.loop(0, chunks)
+    @pl.loop(0, chunks // 2)
     def _(r):
-        held = pl.ds(pl.multiple_of(PAD + 8 * r, 8), 8)
+        held = pl.ds(pl.multiple_of(PAD + 16 * r, 8), 16)
         vals = [st[c, held, :] for c in range(FIELDS)]
         for c in range(FIELDS):
-            outs[c // LEVELS][c % LEVELS, pl.ds(pl.multiple_of(8 * r, 8), 8), :] = vals[c]
+            outs[c // LEVELS][c % LEVELS, pl.ds(pl.multiple_of(16 * r, 16), 16), :] = vals[c]
 
     to_east.wait_send()
     to_west.wait_send()

time: 18 us -> 17.2 us (0.956)
  Pallas kernels: 17.2 us -> 16.4 us
    pallas_call x1, Pallas kernels: 16.3 us -> 15.5 us  [shards(): pl.pallas_call(functools.partial(kernel, nlon, nlat, rows, cols), out_sha...]
where the time goes in v7:
time: 17.2 us; the launch traced here: 17.1 us
  Pallas kernels  16.4 us (95%)
  between operations  0.64 us (4%)
    pallas_call x1, Pallas kernels, shards(): pl.pallas_call(functools.partial(kernel, nlon, nlat, rows, cols), out_sha...  15.5 us
    pallas_call x1, Pallas kernels, shards(): pl.pallas_call(hand_over, out_shape=out_shape, in_specs=[pl.BlockSpec(mem...  0.91 us

profile of v7, /device:TPU:0, one launch (start us, length us, event | category | flops | bytes accessed | tf_op | source)
XLA Modules:
  0.0 17.1 jit_solution(17118259328984286522)
XLA Ops:
  0.6 15.5 %shard_map.147 = (f32[4,96,128]{2,1,0:T(8,128)S(1)}, f32[4,96,128]{2,1,0:T(8,128)S(1)}, f32[4,96,128]{2,1,0:T(8,128)S(1)}, f32[4,96,128]{2,1,0:T(8,128)S(1)}) custom-call(f32[4,96,128]{2,1,0:T(8,128)} %refs_0_.1, f32[4,96,128]{2,1,0:T(8,128)} %refs_1_.1, f32[4,96,128]{2,1,0:T(8,128)} %refs_2_.1, f32[4,96,128]{2,1,0:T(8,128)} %refs_3_.1, ...), custom_call_target="tpu_custom_call" | custom-call | tf_op jit(solution)/shard_map/pallas_call | solution.py:443
  16.2 0.9 %shard_map.148 = (f32[4,96,128]{2,1,0:T(8,128)}, f32[4,96,128]{2,1,0:T(8,128)}, f32[4,96,128]{2,1,0:T(8,128)}, f32[4,96,128]{2,1,0:T(8,128)}) custom-call(f32[4,96,128]{2,1,0:T(8,128)S(1)} %get-tuple-element.8.refs_0_, f32[4,96,128]{2,1,0:T(8,128)S(1)} %get-tuple-element.9.refs_1_, f32[4,96,128]{2,1,0:T(8,128)S(1)} %get-tuple-element.10.refs_2_, ...), custom_call_target="tpu_custom_call" | custom-call | tf_op jit(solution)/shard_map/pallas_call | solution.py:467

commit v8 on v7

--- a/solution.py
+++ b/solution.py
@@ -132,9 +132,8 @@
                 st[at, held, :] = val
 
     def entries(load, save):
-        @pl.loop(0, ENTRIES // 4)
-        def _(g):
-            at = 4 * g + FIELDS * (g >= FIELDS // 4).astype(jnp.int32)
+        for g in range(ENTRIES // 4):
+            at = 4 * g + (FIELDS if g >= FIELDS // 4 else 0)
             held = [load(4 * g + i, at + i) for i in range(4)]
             for i in range(4):
                 save(4 * g + i, at + i, *held[i])
@@ -281,8 +280,7 @@
         )
 
     def between():
-        @pl.loop(0, 5 * LEVELS // 4)
-        def _(g):
+        for g in range(5 * LEVELS // 4):
             held = [(st[FIELDS + 4 * g + i, pl.ds(row0, 8), :], st[FIELDS + 4 * g + i, pl.ds(col0, 8), :]) for i in range(4)]
             for i, (about_row, about_col) in enumerate(held):
                 c = 4 * g + i

time: 17.2 us -> 17.2 us (level)
  no operation moved by 1% of the time
where the time goes in v8:
time: 17.2 us; the launch traced here: 17 us
  Pallas kernels  16.4 us (95%)
  between operations  0.64 us (4%)
    pallas_call x1, Pallas kernels, shards(): pl.pallas_call(functools.partial(kernel, nlon, nlat, rows, cols), out_sha...  15.4 us
    pallas_call x1, Pallas kernels, shards(): pl.pallas_call(hand_over, out_shape=out_shape, in_specs=[pl.BlockSpec(mem...  0.91 us

profile of v8, /device:TPU:0, one launch (start us, length us, event | category | flops | bytes accessed | tf_op | source)
XLA Modules:
  0.0 17.0 jit_solution(3613974103824100533)
XLA Ops:
  0.6 15.4 %shard_map.147 = (f32[4,96,128]{2,1,0:T(8,128)S(1)}, f32[4,96,128]{2,1,0:T(8,128)S(1)}, f32[4,96,128]{2,1,0:T(8,128)S(1)}, f32[4,96,128]{2,1,0:T(8,128)S(1)}) custom-call(f32[4,96,128]{2,1,0:T(8,128)} %refs_0_.1, f32[4,96,128]{2,1,0:T(8,128)} %refs_1_.1, f32[4,96,128]{2,1,0:T(8,128)} %refs_2_.1, f32[4,96,128]{2,1,0:T(8,128)} %refs_3_.1, ...), custom_call_target="tpu_custom_call" | custom-call | tf_op jit(solution)/shard_map/pallas_call | solution.py:441
  16.1 0.9 %shard_map.148 = (f32[4,96,128]{2,1,0:T(8,128)}, f32[4,96,128]{2,1,0:T(8,128)}, f32[4,96,128]{2,1,0:T(8,128)}, f32[4,96,128]{2,1,0:T(8,128)}) custom-call(f32[4,96,128]{2,1,0:T(8,128)S(1)} %get-tuple-element.8.refs_0_, f32[4,96,128]{2,1,0:T(8,128)S(1)} %get-tuple-element.9.refs_1_, f32[4,96,128]{2,1,0:T(8,128)S(1)} %get-tuple-element.10.refs_2_, ...), custom_call_target="tpu_custom_call" | custom-call | tf_op jit(solution)/shard_map/pallas_call | solution.py:465
